TPU v7x, 32 devices: a whole 2x2x4 slice. The times are simulated.
32 devices in a mesh: seq: 8 (over z, x), dp: 4 (over y, core).
Axes of the slice: x: 2, y: 2, z: 4, core: 2. Of those that a mesh axis runs over, the one named last changes fastest.
Arguments:
- hidden_in: bfloat16 [8, 2048, 768], P('dp', 'seq'), may hold values from -6 to 6
- cotangent: bfloat16 [8, 2048, 768], P('dp', 'seq'), may hold values from -6 to 6
- w_qkv: float32 [768, 2304], P('dp'), may hold values from -0.3125 to 0.3125
- w_out: float32 [768, 768], P('dp'), may hold values from -0.75 to 0.75
- pool_kernel: float32 [2, 5, 768], replicated, may hold values from -3 to 3
- norm1_gain: float32 [768], replicated, may hold values from 0.5 to 1.5
- norm1_bias: float32 [768], replicated, may hold values from -1.5 to 1.5
- w_up: float32 [768, 3072], P('dp'), may hold values from -0.21875 to 0.21875
- up_bias: float32 [3072], replicated, may hold values from -2.5 to 2.5
- w_down: float32 [3072, 768], P('dp'), may hold values from -0.15625 to 0.15625
- down_bias: float32 [768], replicated, may hold values from -1.5 to 1.5
- norm2_gain: float32 [768], replicated, may hold values from 0.5 to 1.5
- norm2_bias: float32 [768], replicated, may hold values from -1.5 to 1.5
- doc_lengths: int32 [8, 2], P('dp'), may hold values from 0 to 2048, as said below
- doc_offsets: int32 [8, 2], P('dp'), may hold values from 0 to 2048, as said below
Outputs:
- block_out: float32 [8, 2048, 768], P('dp', 'seq')
- grad_in: float32 [8, 2048, 768], P('dp', 'seq')
- grad_w_qkv: float32 [768, 2304], P('dp')
- grad_w_out: float32 [768, 768], P('dp')
- grad_pool_kernel: float32 [2, 5, 768], replicated
- grad_norm1_gain: float32 [768], replicated
- grad_norm1_bias: float32 [768], replicated
- grad_w_up: float32 [768, 3072], P('dp')
- grad_up_bias: float32 [3072], replicated
- grad_w_down: float32 [3072, 768], P('dp')
- grad_down_bias: float32 [768], replicated
- grad_norm2_gain: float32 [768], replicated
- grad_norm2_bias: float32 [768], replicated
Inputs may be any that keep to these rules, and one draw needn't show every extreme that they name: Slot j of a row gives document j: it occupies tokens doc_offsets[j] to doc_offsets[j] + doc_lengths[j] - 1 of the row. Lengths are multiples of 4; documents lie in rising order without intersection, each starts at a multiple of 128, the first at 0; an unused slot has length 0 and offset 2048. Of the 2 rows of each index of dp, one is a single document of 2048 tokens. `doc_offsets`: the starts of the documents given by doc_lengths.
All inputs are finite; a program needn't handle non-finite values.
Results may differ from a plain program's by a relative error of at most 0.018.
The roundings to bfloat16 on the way count: a program that leaves them out, or rounds other values in their place, can miss the bound.
Values may be sent and summed in bfloat16 or wider, within the bound.
No kernel may reach another device: no remote copies, remote signals or barrier semaphores. Data moves between devices by JAX's collectives and lax.ppermute only.
A program may use at most 192 MiB of HBM per device.

v0:
```python
from functools import partial

import jax
import jax.numpy as jnp
from jax import lax
from jax.sharding import PartitionSpec as P

HEAD = 64
WIN = 128
PWIN = 512


epsilon = 1e-05


def extended(cells, sides, width):
    for axis, dim in sides:
        count = lax.axis_size(axis)
        ends = count - 1
        head = lax.slice_in_dim(cells, 0, width, axis=dim)
        tail = lax.slice_in_dim(cells, cells.shape[dim] - width, cells.shape[dim], axis=dim)
        cells = jnp.concatenate(
            [
                lax.ppermute(tail, axis, [(i, (i + 1) % count) for i in range(ends)]),
                cells,
                lax.ppermute(head, axis, [((i + 1) % count, i) for i in range(ends)]),
            ],
            axis=dim,
        )
    return cells


def segment_ids(places, doc_start, doc_len, seq_len):
    expanded = places[..., None]
    started = jnp.sum((doc_start <= expanded).astype(jnp.int32), axis=-1)
    inside = jnp.sum(
        ((doc_start <= expanded) & (expanded < doc_start + doc_len)).astype(jnp.int32), axis=-1
    )
    segment = 2 * started + 1 - inside
    return jnp.where((places >= 0) & (places < seq_len), segment, -1)


def norm_forward(values, gain_vec, bias_vec):
    centered = values - jnp.mean(values, axis=-1, keepdims=True)
    inv_spread = lax.rsqrt(jnp.mean(centered * centered, axis=-1, keepdims=True) + epsilon)
    unit_vals = centered * inv_spread
    return (unit_vals * gain_vec + bias_vec, unit_vals, inv_spread)


def norm_backward(grad_out, unit_vals, inv_spread, gain_vec):
    grad_unit = grad_out * gain_vec
    grad_values = inv_spread * (
        grad_unit
        - jnp.mean(grad_unit, axis=-1, keepdims=True)
        - unit_vals * jnp.mean(grad_unit * unit_vals, axis=-1, keepdims=True)
    )
    return (grad_values, jnp.sum(grad_out * unit_vals, axis=(0, 1)), jnp.sum(grad_out, axis=(0, 1)))


def scores_of(queries, key_rows, allowed):
    products = (
        jnp.einsum("rqhd,rkhd->rhqk", queries, key_rows, preferred_element_type=jnp.float32) * 0.125
    )
    return jnp.where(allowed[:, None], products, -1e30)


def attend_forward(queries, key_rows, value_rows, allowed):
    scores = scores_of(queries, key_rows, allowed)
    highest = jnp.max(scores, axis=-1, keepdims=True)
    exponent = jnp.exp(scores - highest)
    normalizer = jnp.sum(exponent, axis=-1, keepdims=True)
    shares = (exponent / normalizer).astype(jnp.bfloat16)
    result = jnp.einsum("rhqk,rkhd->rqhd", shares, value_rows, preferred_element_type=jnp.float32)
    return (result, highest + jnp.log(normalizer))


def attend_backward(queries, key_rows, value_rows, allowed, log_total, grad_result):
    scores = scores_of(queries, key_rows, allowed)
    shares = jnp.where(allowed[:, None], jnp.exp(scores - log_total), 0.0)
    grad_shares = jnp.einsum(
        "rqhd,rkhd->rhqk", grad_result, value_rows, preferred_element_type=jnp.float32
    )
    row_inner = jnp.sum(shares * grad_shares, axis=-1, keepdims=True)
    grad_scores = (shares * (grad_shares - row_inner)).astype(jnp.bfloat16)
    grad_query = (
        jnp.einsum("rhqk,rkhd->rqhd", grad_scores, key_rows, preferred_element_type=jnp.float32)
        * 0.125
    )
    grad_key = (
        jnp.einsum("rhqk,rqhd->rkhd", grad_scores, queries, preferred_element_type=jnp.float32)
        * 0.125
    )
    grad_value = jnp.einsum(
        "rhqk,rqhd->rkhd",
        shares.astype(jnp.bfloat16),
        grad_result,
        preferred_element_type=jnp.float32,
    )
    return (grad_query, grad_key, grad_value)


def placed(block_part, before):
    return jnp.pad(block_part, ((0, 0), (before, 1 - before), (0, 0)))


def local(
    hidden_in,
    cotangent,
    w_qkv,
    w_out,
    pool_kernel,
    norm1_gain,
    norm1_bias,
    w_up,
    up_bias,
    w_down,
    down_bias,
    norm2_gain,
    norm2_bias,
    doc_lengths,
    doc_offsets,
):
    full_qkv, full_out, full_up, full_down = (
        lax.all_gather(w_qkv.astype(jnp.bfloat16), "dp", axis=0, tiled=True),
        lax.all_gather(w_out.astype(jnp.bfloat16), "dp", axis=0, tiled=True),
        lax.all_gather(w_up.astype(jnp.bfloat16), "dp", axis=0, tiled=True),
        lax.all_gather(w_down.astype(jnp.bfloat16), "dp", axis=0, tiled=True),
    )
    row_count, tok_count, model_width = hidden_in.shape
    head_count = model_width // HEAD
    seq_len = tok_count * lax.axis_size("seq")
    anchor = lax.axis_index("seq") * tok_count
    half_win = WIN // 2
    pool_span = PWIN // 2
    pool_reach = pool_span // 4
    pooled_count = tok_count // 4
    doc_start = doc_offsets[:, None, :]
    doc_len = doc_lengths[:, None, :]

    def segments_at(places):
        return segment_ids(
            jnp.broadcast_to(places, (row_count, places.shape[0])), doc_start, doc_len, seq_len
        )

    q_place = anchor + jnp.arange(tok_count, dtype=jnp.int32)
    near_place = anchor - half_win + jnp.arange(tok_count + 2 * half_win, dtype=jnp.int32)
    far_place = 4 * (
        anchor // 4 - pool_reach + jnp.arange(pooled_count + 2 * pool_reach, dtype=jnp.int32)
    )
    q_seg = segments_at(q_place)
    near_seg = segments_at(near_place)
    far_seg = segments_at(far_place)
    near_gap = near_place[None, :] - q_place[:, None]
    far_gap = far_place[None, :] - q_place[:, None]
    near_ok = (
        (near_seg[:, None, :] == q_seg[:, :, None])
        & (near_gap >= -half_win)
        & (near_gap < half_win)
    )
    far_ok = (
        (far_seg[:, None, :] == q_seg[:, :, None]) & (far_gap >= -pool_span) & (far_gap < pool_span)
    )

    def split_heads(tensor):
        return tensor.reshape(tensor.shape[0], tensor.shape[1], head_count, HEAD)

    mixed_qkv = jnp.einsum(
        "rtd,de->rte", hidden_in, full_qkv, preferred_element_type=jnp.float32
    ).astype(jnp.bfloat16)
    queries = mixed_qkv[..., :model_width]
    keyvals = mixed_qkv[..., model_width:]
    near_kv = extended(keyvals, (("seq", 1),), half_win)
    centers = q_seg[:, ::4]
    tap_weights = jnp.concatenate([pool_kernel[0], pool_kernel[1]], axis=-1)
    tap_values = []
    tap_ok = []
    pooled = jnp.zeros((row_count, pooled_count, 2 * model_width), jnp.float32)
    for tap_index in range(5):
        tap_start = half_win - 2 + tap_index
        tap_rows = near_kv[:, tap_start : tap_start + tok_count].reshape(
            row_count, pooled_count, 4, 2 * model_width
        )[:, :, 0]
        seg_taken = near_seg[:, tap_start : tap_start + tok_count].reshape(
            row_count, pooled_count, 4
        )[:, :, 0]
        tap_valid = seg_taken == centers
        tap_values.append(tap_rows)
        tap_ok.append(tap_valid)
        pooled = (
            pooled
            + jnp.where(tap_valid[..., None], tap_rows.astype(jnp.float32), 0.0)
            * tap_weights[tap_index]
        )
    far_kv = extended(pooled.astype(jnp.bfloat16), (("seq", 1),), pool_reach)
    q_heads = split_heads(queries)
    near_k = split_heads(near_kv[..., :model_width])
    near_v = split_heads(near_kv[..., model_width:])
    far_k = split_heads(far_kv[..., :model_width])
    far_v = split_heads(far_kv[..., model_width:])
    near_result, near_log = attend_forward(q_heads, near_k, near_v, near_ok)
    far_result, far_log = attend_forward(q_heads, far_k, far_v, far_ok)
    attended = (
        (near_result + far_result).reshape(row_count, tok_count, model_width).astype(jnp.bfloat16)
    )
    branch = jnp.einsum("rtd,de->rte", attended, full_out, preferred_element_type=jnp.float32)
    normed, unit_one, scale_one = norm_forward(
        hidden_in.astype(jnp.float32) + branch, norm1_gain, norm1_bias
    )
    normed_b = normed.astype(jnp.bfloat16)
    pre_act = (
        jnp.einsum("rtd,df->rtf", normed_b, full_up, preferred_element_type=jnp.float32) + up_bias
    )
    activated, gelu_back = jax.vjp(partial(jax.nn.gelu, approximate=False), pre_act)
    activated_b = activated.astype(jnp.bfloat16)
    second = (
        jnp.einsum("rtf,fd->rtd", activated_b, full_down, preferred_element_type=jnp.float32)
        + down_bias
    )
    block_out, unit_two, scale_two = norm_forward(normed + second, norm2_gain, norm2_bias)
    grad_sum2, grad_gain2, grad_bias2 = norm_backward(
        cotangent.astype(jnp.float32), unit_two, scale_two, norm2_gain
    )
    grad_second = grad_sum2.astype(jnp.bfloat16)
    grad_down_local = jnp.sum(grad_second.astype(jnp.float32), axis=(0, 1))
    term_down = jnp.einsum(
        "rtf,rtd->fd", activated_b, grad_second, preferred_element_type=jnp.float32
    )
    grad_act = jnp.einsum("rtd,fd->rtf", grad_second, full_down, preferred_element_type=jnp.float32)
    (grad_pre,) = gelu_back(grad_act)
    grad_pre_b = grad_pre.astype(jnp.bfloat16)
    grad_up_local = jnp.sum(grad_pre_b.astype(jnp.float32), axis=(0, 1))
    term_up = jnp.einsum("rtd,rtf->df", normed_b, grad_pre_b, preferred_element_type=jnp.float32)
    grad_normed = grad_sum2 + jnp.einsum(
        "rtf,df->rtd", grad_pre_b, full_up, preferred_element_type=jnp.float32
    )
    grad_sum1, grad_gain1, grad_bias1 = norm_backward(grad_normed, unit_one, scale_one, norm1_gain)
    grad_branch = grad_sum1.astype(jnp.bfloat16)
    term_out = jnp.einsum("rtd,rte->de", attended, grad_branch, preferred_element_type=jnp.float32)
    grad_att = jnp.einsum(
        "rte,de->rtd", grad_branch, full_out, preferred_element_type=jnp.float32
    ).astype(jnp.bfloat16)
    grad_att_heads = split_heads(grad_att)
    near_dq, near_dk, near_dv = attend_backward(
        q_heads, near_k, near_v, near_ok, near_log, grad_att_heads
    )
    far_dq, far_dk, far_dv = attend_backward(q_heads, far_k, far_v, far_ok, far_log, grad_att_heads)
    grad_near = jnp.concatenate(
        [near_dk.reshape(row_count, -1, model_width), near_dv.reshape(row_count, -1, model_width)],
        axis=-1,
    )
    grad_far = jnp.concatenate(
        [far_dk.reshape(row_count, -1, model_width), far_dv.reshape(row_count, -1, model_width)],
        axis=-1,
    )
    far_outgoing = jnp.concatenate([grad_far[:, :pool_reach], grad_far[:, -pool_reach:]], axis=1)
    far_incoming = extended(far_outgoing.astype(jnp.bfloat16), (("seq", 1),), pool_reach).astype(
        far_outgoing.dtype
    )
    grad_pooled = (
        grad_far[:, pool_reach : pool_reach + pooled_count]
        + far_incoming[:, :pool_reach]
        + far_incoming[:, -pool_reach:]
    )
    tap_parts = []
    kernel_grad = []
    for tap_index in range(5):
        masked = jnp.where(tap_ok[tap_index][..., None], grad_pooled, 0.0)
        tap_parts.append(masked * tap_weights[tap_index])
        kernel_grad.append(jnp.sum(masked * tap_values[tap_index].astype(jnp.float32), axis=(0, 1)))
    stacked = jnp.stack(
        [
            placed(tap_parts[2], 1),
            placed(tap_parts[3], 1),
            placed(tap_parts[0], 0) + placed(tap_parts[4], 1),
            placed(tap_parts[1], 0),
        ],
        axis=2,
    )
    spread_back = stacked.reshape(row_count, tok_count + 4, 2 * model_width)
    grad_near = grad_near + jnp.pad(spread_back, ((0, 0), (half_win - 4, half_win), (0, 0)))
    pool_grad = jnp.stack(kernel_grad).reshape(5, 2, model_width).transpose(1, 0, 2)
    near_outgoing = jnp.concatenate([grad_near[:, :half_win], grad_near[:, -half_win:]], axis=1)
    near_incoming = extended(near_outgoing.astype(jnp.bfloat16), (("seq", 1),), half_win).astype(
        near_outgoing.dtype
    )
    grad_kv = (
        grad_near[:, half_win : half_win + tok_count]
        + jnp.pad(near_incoming[:, :half_win], ((0, 0), (0, tok_count - half_win), (0, 0)))
        + jnp.pad(near_incoming[:, -half_win:], ((0, 0), (tok_count - half_win, 0), (0, 0)))
    )
    grad_query = (near_dq + far_dq).reshape(row_count, tok_count, model_width)
    grad_mixed = jnp.concatenate([grad_query, grad_kv], axis=-1).astype(jnp.bfloat16)
    term_qkv = jnp.einsum("rtd,rte->de", hidden_in, grad_mixed, preferred_element_type=jnp.float32)
    grad_in = grad_sum1 + jnp.einsum(
        "rte,de->rtd", grad_mixed, full_qkv, preferred_element_type=jnp.float32
    )
    weight_terms = (term_qkv, term_out, term_up, term_down)
    shares = (
        lax.psum_scatter(
            weight_terms[0].astype(jnp.bfloat16), "dp", scatter_dimension=0, tiled=True
        ).astype(jnp.float32),
        lax.psum_scatter(
            weight_terms[1].astype(jnp.bfloat16), "dp", scatter_dimension=0, tiled=True
        ).astype(jnp.float32),
        lax.psum_scatter(
            weight_terms[2].astype(jnp.bfloat16), "dp", scatter_dimension=0, tiled=True
        ).astype(jnp.float32),
        lax.psum_scatter(
            weight_terms[3].astype(jnp.bfloat16), "dp", scatter_dimension=0, tiled=True
        ).astype(jnp.float32),
    )
    finals = lax.psum((shares[0], shares[1], shares[2], shares[3]), "seq")
    smalls = lax.psum(
        (pool_grad, grad_gain1, grad_bias1, grad_up_local, grad_down_local, grad_gain2, grad_bias2),
        ("seq", "dp"),
    )
    return (
        block_out,
        grad_in,
        finals[0],
        finals[1],
        smalls[0],
        smalls[1],
        smalls[2],
        finals[2],
        smalls[3],
        finals[3],
        smalls[4],
        smalls[5],
        smalls[6],
    )


def solution(mesh):
    placed = (
        P("dp", "seq", None),
        P("dp", "seq", None),
        P("dp", None),
        P("dp", None),
        P(),
        P(),
        P(),
        P("dp", None),
        P(),
        P("dp", None),
        P(),
        P(),
        P(),
        P("dp", None),
        P("dp", None),
    )
    return jax.shard_map(
        local,
        mesh=mesh,
        in_specs=placed,
        out_specs=(
            P("dp", "seq", None),
            P("dp", "seq", None),
            P("dp", None),
            P("dp", None),
            P(),
            P(),
            P(),
            P("dp", None),
            P(),
            P("dp", None),
            P(),
            P(),
            P(),
        ),
        check_vma=False,
    )
```

profile of v0, /device:TPU:0, one launch (start us, length us, event | category | flops | bytes accessed | tf_op | source)
XLA Modules:
  0.0 771.8 jit_solution(11684696706635984204)
XLA Ops:
  18.4 25.4 %all-gather.5.cloned.1.call-done = bf16[768,2304]{1,0:T(8,128)(2,1)} async-done(((bf16[192,2304]{1,0:T(8,128)(2,1)}), bf16[768,2304]{1,0:T(8,128)(2,1)}) %all-gather.5.cloned.1.call-update) | async-done | bytes 3538960 | tf_op jit(solution)/shard_map/all_gather | solution.py:124
  50.0 5.4 collective-permute-start
  62.1 8.2 %collective-permute-done = bf16[2,64,1536]{2,1,0:T(8,128)(2,1)} collective-permute-done((bf16[2,64,1536]{2,1,0:T(8,128)(2,1)}, bf16[2,64,1536]{2,1,0:T(8,128)(2,1)}, u32[]{:S(2)}, u32[]{:S(2)}) %collective-permute-start) | collective-permute-done | bytes 393248 | tf_op jit(solution)/shard_map/ppermute | solution.py:24
  100.8 6.1 fusion.72
  108.2 5.7 collective-permute-start.2
  149.0 7.0 fusion.43
  158.7 15.7 %multiply_convert_fusion.1 = (bf16[2,256,3072]{2,1,0:T(8,128)(2,1)}, f32[2,256,3072]{2,1,0:T(8,128)}) fusion(f32[2,256,3072]{2,1,0:T(8,128)S(1)} %get-tuple-element.166, f32[3072]{0:T(1024)S(1)} %copy-done.72, u8[256,3072]{1,0:T(8,128)(4,1)S(1)} %get-tuple-element.79, u8[256,3072]{1,0:T(8,128)(4,1)S(1)} %get-tuple-element.78), kind=kLoop, calls=%fused_computation.19 | loop fusion | flops 111673344 | bytes 17313792 | tf_op jit(solution)/shard_map/convert_element_type | solution.py:214
  174.4 6.2 fusion.118
  184.8 8.9 %convert_reduce_fusion = (f32[3072]{0:T(1024)}, bf16[2,256,3072]{2,1,0:T(8,128)(2,1)}) fusion(f32[2,256,3072]{2,1,0:T(8,128)S(1)} %copy-done.19, bf16[2,256,768]{2,1,0:T(8,128)(2,1)S(1)} %get-tuple-element.116, bf16[3072,768]{1,0:T(8,128)(2,1)} %all-gather.11.cloned.1.call-done, f32[2,256,3072]{2,1,0:T(8,128)S(1)} %copy-done.18, f32[3072]{0:T(1024)S(1)} %copy-done.72), kind=kOutput, calls=%fused_computation.17 | convolution fusion | flops 2442654720 | bytes 21258240 | tf_op jit(solution)/shard_map/rtd,fd->rtf/dot_general | solution.py:228
  193.7 7.2 multiply_reduce_fusion.2
  212.9 7.1 multiply_reduce_fusion.1
  224.1 6.5 multiply_reduce_fusion
  232.5 5.2 multiply_convert_fusion.2
  246.4 5.4 collective-permute-start.4
  253.1 8.0 %multiply_convert_fusion = bf16[2,12,256,384]{3,2,1,0:T(8,128)(2,1)S(1)} fusion(f32[2,12,256,384]{3,2,1,0:T(8,128)} %get-tuple-element.173, f32[2,12,256]{2,1,0:T(8,128)S(1)} %get-tuple-element.172, f32[2,12,256]{2,1,0:T(8,128)S(1)} %log_add_fusion.1, f32[2,12,256,384]{3,2,1,0:T(8,128)} %copy-done, pred[2,256,384]{2,1,0:T(8,128)(4,1)S(1)} %and_and_fusion), kind=kLoop, calls=%fused_computation.3 | loop fusion | flops 16515072 | bytes 23838720 | tf_op jit(solution)/shard_map/convert_element_type | solution.py:84
  272.4 10.8 %fusion.68 = (f32[1536]{0:T(1024)}, f32[1536]{0:T(1024)}, f32[1536]{0:T(1024)}, f32[1536]{0:T(1024)}, f32[1536]{0:T(1024)}, /*index=5*/f32[2,64,1536]{2,0,1:T(2,128)S(1)}) fusion(pred[2,64]{0,1:T(8,128)(4,1)S(1)} %copy.167, bf16[2,64,1,1536]{3,2,1,0:T(2,128)(2,1)S(1)} %copy-done.14, bf16[2,64,1,1536]{3,2,1,0:T(2,128)(2,1)S(1)} %copy-done.15, ...), kind=kLoop, calls=%fused_computation.144 | loop fusion | flops 6087168 | bytes 6716032 | tf_op jit(solution)/shard_map/reduce_sum | solution.py:269
  299.9 12.2 %collective-permute-done.6 = bf16[2,64,1536]{2,1,0:T(8,128)(2,1)S(1)} collective-permute-done((bf16[2,64,1536]{2,1,0:T(8,128)(2,1)S(1)}, bf16[2,64,1536]{2,1,0:T(8,128)(2,1)S(1)}, u32[]{:S(2)}, u32[]{:S(2)}) %collective-permute-start.6) | collective-permute-done | bytes 393248 | tf_op jit(solution)/shard_map/ppermute | solution.py:24
  323.6 6.5 bitcast_convert_fusion.1
  332.5 5.6 bitcast_convert_fusion
  339.0 41.9 %all-reduce.7 = (f32[2,5,768]{2,0,1:T(2,128)}, f32[768]{0:T(1024)}, f32[768]{0:T(1024)}, f32[3072]{0:T(1024)}, f32[768]{0:T(1024)}, /*index=5*/f32[768]{0:T(1024)}, f32[768]{0:T(1024)}) all-reduce(f32[2,5,768]{2,0,1:T(2,128)S(1)} %bitcast.190, f32[768]{0:T(1024)S(1)} %copy-done.76, ...), channel_id=1, replica_groups=mesh['seq'=8,'dp'=4] {'seq','dp'}, use_global_device_ids=true, to_apply=%region_29.30 | all-reduce | flops 14592 | bytes 116736 | tf_op jit(solution)/shard_map/psum | solution.py:313
  380.8 5.4 fusion.44
  387.8 26.2 %reduce-scatter.9.cloned.1.call-done = bf16[192,3072]{1,0:T(8,128)(2,1)} async-done(((bf16[768,3072]{1,0:T(8,128)(2,1)}), bf16[192,3072]{1,0:T(8,128)(2,1)}) %reduce-scatter.9.cloned.1.call-update) | async-done | bytes 1179664 | tf_op jit(solution)/shard_map/reduce_scatter | solution.py:305
  414.0 50.6 %reduce-scatter.11.cloned.1.call-done = bf16[768,768]{1,0:T(8,128)(2,1)} async-done(((bf16[3072,768]{1,0:T(8,128)(2,1)}), bf16[768,768]{1,0:T(8,128)(2,1)}) %reduce-scatter.11.cloned.1.call-update) | async-done | bytes 1179664 | tf_op jit(solution)/shard_map/reduce_scatter | solution.py:308
  464.6 298.4 %all-reduce.10 = (f32[192,2304]{0,1:T(8,128)S(1)}, f32[192,768]{1,0:T(8,128)}, f32[192,3072]{1,0:T(8,128)}, f32[768,768]{1,0:T(8,128)}) all-reduce(bf16[192,2304]{0,1:T(8,128)(2,1)S(1)} %copy.191, bf16[192,768]{1,0:T(8,128)(2,1)} %reduce-scatter.7.cloned.1.call-done, ...), channel_id=1, replica_groups=mesh['seq'=8,'dp'=4] {'seq'}, use_global_device_ids=true, to_apply=%region_21.22 | all-reduce | flops 1769472 | bytes 10616832 | tf_op jit(solution)/shard_map/psum | solution.py:312
  (353 shorter events, 170.3 us)
Async XLA Ops:
  7.2 36.5 %all-gather.5.cloned.1.call-start = ((), (), s32[]{:S(2)}) async-start(), calls=%async_computation.4 | async-start | bytes 4423680 | tf_op jit(solution)/shard_map/all_gather | solution.py:124
  9.9 135.2 %all-gather.7.cloned.1.call-start = ((), (), s32[]{:S(2)}) async-start(), calls=%async_computation.5 | async-start | bytes 1474560 | tf_op jit(solution)/shard_map/all_gather | solution.py:125
  10.8 138.2 %all-gather.9.cloned.1.call-start = ((), (), s32[]{:S(2)}) async-start(), calls=%async_computation.6 | async-start | bytes 5898240 | tf_op jit(solution)/shard_map/all_gather | solution.py:126
  12.0 162.4 %all-gather.11.cloned.1.call-start = ((), (), s32[]{:S(2)}) async-start(), calls=%async_computation.7 | async-start | bytes 5898240 | tf_op jit(solution)/shard_map/all_gather | solution.py:127
  15.0 371.3 %reduce-scatter.7.cloned.1.call-start = ((), (), s32[]{:S(2)}) async-start(), calls=%async_computation.8 | async-start | bytes 1474560 | tf_op jit(solution)/shard_map/reduce_scatter | solution.py:302
  17.2 83.5 %copy-start.42 = (pred[2,64]{0,1:T(8,128)(4,1)}, pred[2,64]{0,1:T(8,128)(4,1)S(1)}, u32[]{:S(2)}) copy-start(pred[2,64]{0,1:T(8,128)(4,1)S(1)} %copy.165) | copy-start | bytes 388
  17.4 83.4 %copy-start.44 = (pred[2,64]{0,1:T(8,128)(4,1)}, pred[2,64]{0,1:T(8,128)(4,1)S(1)}, u32[]{:S(2)}) copy-start(pred[2,64]{0,1:T(8,128)(4,1)S(1)} %copy.163) | copy-start | bytes 388
  17.5 83.2 %copy-start.46 = (pred[2,64]{0,1:T(8,128)(4,1)}, pred[2,64]{0,1:T(8,128)(4,1)S(1)}, u32[]{:S(2)}) copy-start(pred[2,64]{0,1:T(8,128)(4,1)S(1)} %copy.161) | copy-start | bytes 388
  18.2 82.6 %copy-start.48 = (f32[1536]{0:T(1024)}, f32[1536]{0:T(1024)S(1)}, u32[]{:S(2)}) copy-start(f32[1536]{0:T(1024)S(1)} %get-tuple-element.93) | copy-start | bytes 18436
  18.2 82.6 %copy-start.50 = (f32[1536]{0:T(1024)}, f32[1536]{0:T(1024)S(1)}, u32[]{:S(2)}) copy-start(f32[1536]{0:T(1024)S(1)} %get-tuple-element.94) | copy-start | bytes 18436
  48.7 13.5 %collective-permute-start.1 = (bf16[2,64,1536]{2,1,0:T(8,128)(2,1)}, bf16[2,64,1536]{2,1,0:T(8,128)(2,1)}, u32[]{:S(2)}, u32[]{:S(2)}) collective-permute-start(bf16[2,64,1536]{2,1,0:T(8,128)(2,1)} %get-tuple-element.126), channel_id=1, source_target_pairs={{4,0},{8,4},{12,8},{16,12},{20,16},{24,20},{28,24},{5,1},{9,5},{13... | collective-permute-start | bytes 1179656 | tf_op jit(solution)/shard_map/ppermute | solution.py:26
  50.0 20.4 %collective-permute-start = (bf16[2,64,1536]{2,1,0:T(8,128)(2,1)}, bf16[2,64,1536]{2,1,0:T(8,128)(2,1)}, u32[]{:S(2)}, u32[]{:S(2)}) collective-permute-start(bf16[2,64,1536]{2,1,0:T(8,128)(2,1)} %get-tuple-element.127), channel_id=1, source_target_pairs={{0,4},{4,8},{8,12},{12,16},{16,20},{20,24},{24,28},{1,5},{5,9},{9,... | collective-permute-start | bytes 1179656 | tf_op jit(solution)/shard_map/ppermute | solution.py:24
  106.9 18.4 %collective-permute-start.3 = (bf16[2,64,1536]{2,0,1:T(2,128)(2,1)}, bf16[2,64,1536]{2,0,1:T(2,128)(2,1)}, u32[]{:S(2)}, u32[]{:S(2)}) collective-permute-start(bf16[2,64,1536]{2,0,1:T(2,128)(2,1)} %fusion.72), channel_id=1, source_target_pairs={{4,0},{8,4},{12,8},{16,12},{20,16},{24,20},{28,24},{5,1},{9,5},{13... | collective-permute-start | bytes 1179656 | tf_op jit(solution)/shard_map/ppermute | solution.py:26
  108.2 21.0 %collective-permute-start.2 = (bf16[2,64,1536]{2,0,1:T(2,128)(2,1)}, bf16[2,64,1536]{2,0,1:T(2,128)(2,1)}, u32[]{:S(2)}, u32[]{:S(2)}) collective-permute-start(bf16[2,64,1536]{2,0,1:T(2,128)(2,1)} %fusion.72), channel_id=1, source_target_pairs={{0,4},{4,8},{8,12},{12,16},{16,20},{20,24},{24,28},{1,5},{5,9},{9,... | collective-permute-start | bytes 1179656 | tf_op jit(solution)/shard_map/ppermute | solution.py:24
  147.7 46.0 %copy-start.22 = (f32[2,256,768]{2,1,0:T(8,128)}, f32[2,256,768]{2,1,0:T(8,128)S(1)}, u32[]{:S(2)}) copy-start(f32[2,256,768]{2,1,0:T(8,128)S(1)} %get-tuple-element.165) | copy-start | bytes 4718596
  230.6 155.7 %reduce-scatter.13.cloned.1.call-start = ((), (), s32[]{:S(2)}) async-start(), calls=%async_computation.11 | async-start | bytes 4423680
  246.4 24.4 %collective-permute-start.4 = (bf16[2,64,1536]{2,0,1:T(2,128)(2,1)}, bf16[2,64,1536]{2,0,1:T(2,128)(2,1)}, u32[]{:S(2)}, u32[]{:S(2)}) collective-permute-start(bf16[2,64,1536]{2,0,1:T(2,128)(2,1)} %get-tuple-element.135), channel_id=1, source_target_pairs={{0,4},{4,8},{8,12},{12,16},{16,20},{20,24},{24,28},{1,5},{5,9},{9,... | collective-permute-start | bytes 1179656 | tf_op jit(solution)/shard_map/ppermute | solution.py:24
  251.8 19.0 %collective-permute-start.5 = (bf16[2,64,1536]{2,0,1:T(2,128)(2,1)}, bf16[2,64,1536]{2,0,1:T(2,128)(2,1)}, u32[]{:S(2)}, u32[]{:S(2)}) collective-permute-start(bf16[2,64,1536]{2,0,1:T(2,128)(2,1)} %get-tuple-element.136), channel_id=1, source_target_pairs={{4,0},{8,4},{12,8},{16,12},{20,16},{24,20},{28,24},{5,1},{9,5},{13... | collective-permute-start | bytes 1179656 | tf_op jit(solution)/shard_map/ppermute | solution.py:26
  291.2 20.9 %collective-permute-start.6 = (bf16[2,64,1536]{2,1,0:T(8,128)(2,1)S(1)}, bf16[2,64,1536]{2,1,0:T(8,128)(2,1)S(1)}, u32[]{:S(2)}, u32[]{:S(2)}) collective-permute-start(bf16[2,64,1536]{2,1,0:T(8,128)(2,1)S(1)} %get-tuple-element.122), channel_id=1, source_target_pairs={{0,4},{4,8},{8,12},{12,16},{16,20},{20,24},{24,28},{1,5},{5,9},{9,... | collective-permute-start | bytes 1179656 | tf_op jit(solution)/shard_map/ppermute | solution.py:24
  295.8 16.3 %collective-permute-start.7 = (bf16[2,64,1536]{2,1,0:T(8,128)(2,1)S(1)}, bf16[2,64,1536]{2,1,0:T(8,128)(2,1)S(1)}, u32[]{:S(2)}, u32[]{:S(2)}) collective-permute-start(bf16[2,64,1536]{2,1,0:T(8,128)(2,1)S(1)} %get-tuple-element.123), channel_id=1, source_target_pairs={{4,0},{8,4},{12,8},{16,12},{20,16},{24,20},{28,24},{5,1},{9,5},{13... | collective-permute-start | bytes 1179656 | tf_op jit(solution)/shard_map/ppermute | solution.py:26
  322.2 91.8 %reduce-scatter.9.cloned.1.call-start = ((), (), s32[]{:S(2)}) async-start(), calls=%async_computation.9 | async-start | bytes 5898240 | tf_op jit(solution)/shard_map/reduce_scatter | solution.py:305
  330.1 134.5 %reduce-scatter.11.cloned.1.call-start = ((), (), s32[]{:S(2)}) async-start(), calls=%async_computation.10 | async-start | bytes 5898240 | tf_op jit(solution)/shard_map/reduce_scatter | solution.py:308
  338.2 42.7 %copy-start.21 = (f32[2,256,768]{2,1,0:T(8,128)S(1)}, f32[2,256,768]{2,1,0:T(8,128)}, u32[]{:S(2)}) copy-start(f32[2,256,768]{2,1,0:T(8,128)} %copy-done.20) | copy-start | bytes 4718596
  338.2 42.7 %copy-start.28 = (bf16[2,256,1536]{2,1,0:T(8,128)(2,1)S(1)}, bf16[2,256,1536]{2,1,0:T(8,128)(2,1)}, u32[]{:S(2)}) copy-start(bf16[2,256,1536]{2,1,0:T(8,128)(2,1)} %copy-done.27) | copy-start | bytes 4718596
  (87 other events, 499.2 us)
Sparse Core Ops, SparseCore 0:
  10.2 33.5 all-gather.4
  45.3 17.4 all-gather.6
  64.3 37.4 all-gather.8
  103.3 37.4 all-gather.10
  230.7 26.0 reduce-scatter.6
  322.3 41.2 reduce-scatter.12
  366.1 47.8 reduce-scatter.8
  416.7 47.8 reduce-scatter.10
where the time goes:
time: 776 us; the launch traced here: 772 us
  blocking collectives  340 us (44%)
  waiting for transfers between devices  129 us (17%)
  matrix products  97.3 us (13%)
  other arithmetic  86.6 us (11%)
  local copies, waits for them, and re-layouts  76 us (10%)
  starting transfers between devices  26.5 us (3%)
  between operations  15.9 us (2%)
    psum x1, blocking collectives, local(): finals = lax.psum((shares[0], shares[1], shares[2], shares[3]), 'seq')  298 us
    reduce_scatter x1, waiting for transfers between devices, local(): lax.psum_scatter(weight_terms[3].astype(jnp.bfloat16), 'dp', scatter_dime...  50.6 us
    psum x1, blocking collectives, local(): lax.psum((pool_grad, grad_gain1, grad_bias1, grad_up_local, grad_down_loc...  41.9 us
    reduce_scatter x1, waiting for transfers between devices, local(): lax.psum_scatter(weight_terms[2].astype(jnp.bfloat16), 'dp', scatter_dime...  26.2 us
    all_gather x1, waiting for transfers between devices, local(): lax.all_gather(w_qkv.astype(jnp.bfloat16), 'dp', axis=0, tiled=True)  25.4 us
    ppermute x4, waiting for transfers between devices, extended(): lax.ppermute(tail, axis, [(i, (i + 1) % count) for i in range(ends)])  24.4 us
    unnamed x197, local copies, waits for them, and re-layouts  21.7 us
    ppermute x4, starting transfers between devices, extended(): lax.ppermute(tail, axis, [(i, (i + 1) % count) for i in range(ends)])  21.1 us
  transfers between devices with their start and end apart: 16, of which 7 were waited for; matrix products, arithmetic and copies ran while one was open for 24% of the time, Pallas kernels for 0%

commit v1 on v0

--- a/solution.py
+++ b/solution.py
@@ -97,6 +97,99 @@
         preferred_element_type=jnp.float32,
     )
     return (grad_query, grad_key, grad_value)
+
+
+def digit_of(axis, stride, radix):
+    return (lax.axis_index(axis) // stride) % radix
+
+
+def shifted(cells, axis, stride, radix, step):
+    pairs = []
+    for i in range(lax.axis_size(axis)):
+        here = (i // stride) % radix
+        pairs.append((i, i + ((here + step) % radix - here) * stride))
+    return lax.ppermute(cells, axis, pairs)
+
+
+def part_of(cells, index):
+    return lax.dynamic_index_in_dim(cells, index, 0, keepdims=False)
+
+
+def scatter_stage(cells, axis, stride, radix):
+    mine = digit_of(axis, stride, radix)
+    received = [
+        shifted(part_of(cells, (mine + k) % radix), axis, stride, radix, k)
+        for k in range(1, radix)
+    ]
+    total = part_of(cells, mine).astype(jnp.float32)
+    for piece in received:
+        total = total + piece.astype(jnp.float32)
+    return total.astype(cells.dtype)
+
+
+def gather_stage(cells, axis, stride, radix):
+    mine = digit_of(axis, stride, radix)
+    got = [cells] + [shifted(cells, axis, stride, radix, radix - k) for k in range(1, radix)]
+    if radix == 2:
+        return jnp.stack(
+            [jnp.where(mine == 0, got[0], got[1]), jnp.where(mine == 0, got[1], got[0])]
+        )
+    return lax.dynamic_slice_in_dim(jnp.stack(got + got), (radix - mine) % radix, radix, 0)
+
+
+def sum_stage(cells, axis, stride, radix):
+    total = cells
+    for k in range(1, radix):
+        total = total + shifted(cells, axis, stride, radix, k)
+    return total
+
+
+def digits_of(count):
+    if count == 8:
+        return [(1, 2), (2, 4)]
+    digits = []
+    stride = 1
+    while stride < count:
+        digits.append((stride, 2))
+        stride *= 2
+    return digits
+
+
+def reduced(cells, dp_first):
+    _, rows, columns = cells.shape
+    seq_digits = digits_of(lax.axis_size("seq"))
+    stride, radix = seq_digits[0]
+    cells = cells.reshape(2, 2, rows, columns).transpose(1, 0, 2, 3)
+    cells = scatter_stage(cells, "dp", 1, 2)
+    if dp_first:
+        cells = scatter_stage(cells, "dp", 2, 2).reshape(radix, rows // radix, columns)
+        cells = scatter_stage(cells, "seq", stride, radix)
+    else:
+        cells = cells.reshape(2, radix, rows // radix, columns).transpose(1, 0, 2, 3)
+        cells = scatter_stage(cells, "seq", stride, radix)
+        cells = scatter_stage(cells, "dp", 2, 2)
+    for stride, radix in seq_digits[1:]:
+        cells = scatter_stage(
+            cells.reshape(radix, cells.shape[0] // radix, columns), "seq", stride, radix
+        )
+    for stride, radix in reversed(seq_digits):
+        cells = gather_stage(cells, "seq", stride, radix).reshape(-1, columns)
+    return cells.astype(jnp.float32)
+
+
+def summed_smalls(parts):
+    flat = jnp.concatenate([part.reshape(-1, 768) for part in parts], axis=0)
+    for stride, radix in ((1, 2), (2, 2)):
+        flat = sum_stage(flat, "dp", stride, radix)
+    for stride, radix in digits_of(lax.axis_size("seq")):
+        flat = sum_stage(flat, "seq", stride, radix)
+    results = []
+    first = 0
+    for part in parts:
+        count = part.size // 768
+        results.append(flat[first : first + count].reshape(part.shape))
+        first += count
+    return results
 
 
 def placed(block_part, before):
@@ -295,24 +388,12 @@
         "rte,de->rtd", grad_mixed, full_qkv, preferred_element_type=jnp.float32
     )
     weight_terms = (term_qkv, term_out, term_up, term_down)
-    shares = (
-        lax.psum_scatter(
-            weight_terms[0].astype(jnp.bfloat16), "dp", scatter_dimension=0, tiled=True
-        ).astype(jnp.float32),
-        lax.psum_scatter(
-            weight_terms[1].astype(jnp.bfloat16), "dp", scatter_dimension=0, tiled=True
-        ).astype(jnp.float32),
-        lax.psum_scatter(
-            weight_terms[2].astype(jnp.bfloat16), "dp", scatter_dimension=0, tiled=True
-        ).astype(jnp.float32),
-        lax.psum_scatter(
-            weight_terms[3].astype(jnp.bfloat16), "dp", scatter_dimension=0, tiled=True
-        ).astype(jnp.float32),
-    )
-    finals = lax.psum((shares[0], shares[1], shares[2], shares[3]), "seq")
-    smalls = lax.psum(
-        (pool_grad, grad_gain1, grad_bias1, grad_up_local, grad_down_local, grad_gain2, grad_bias2),
-        ("seq", "dp"),
+    finals = []
+    for term, dp_first in zip(weight_terms, (True, True, False, True)):
+        term = term.astype(jnp.bfloat16)
+        finals.append(reduced(term.reshape(4, term.shape[0] // 4, term.shape[1]), dp_first))
+    smalls = summed_smalls(
+        (pool_grad, grad_gain1, grad_bias1, grad_up_local, grad_down_local, grad_gain2, grad_bias2)
     )
     return (
         block_out,

time: 776 us -> 521 us (0.67)
  blocking collectives: 340 us -> 0 us
  starting transfers between devices: 26.5 us -> 81.8 us
  waiting for transfers between devices: 129 us -> 144 us
  other arithmetic: 86.6 us -> 98.3 us
  local copies, waits for them, and re-layouts: 76 us -> 86.6 us
  matrix products: 97.3 us -> 89.5 us
    psum x2 -> x0, blocking collectives: 340 us -> none  [the longest x1 298 us: local(): finals = lax.psum((shares[0], shares[1], shares[2], shares[3]), 'seq')]
    ppermute x0 -> x46, waiting for transfers between devices: none -> 108 us  [shifted(): return lax.ppermute(cells, axis, pairs)]
    reduce_scatter x3 -> x0, waiting for transfers between devices: 76.8 us -> none  [the longest x1 50.6 us: local(): lax.psum_scatter(weight_terms[3].astype(jnp.bfloat16), 'dp', scatter_dime...]
    ppermute x0 -> x46, starting transfers between devices: none -> 57.9 us  [shifted(): return lax.ppermute(cells, axis, pairs)]
    convert_element_type x0 -> x16, other arithmetic: none -> 12.9 us  [the longest x12 7.23 us: scatter_stage(): return total.astype(cells.dtype)]
    ppermute x4, waiting for transfers between devices: 24.4 us -> 11.9 us  [extended(): lax.ppermute(tail, axis, [(i, (i + 1) % count) for i in range(ends)])]
    squeeze x0 -> x16, local copies, waits for them, and re-layouts: none -> 8.97 us  [part_of(): return lax.dynamic_index_in_dim(cells, index, 0, keepdims=False)]
    unnamed x197 -> x211, local copies, waits for them, and re-layouts: 21.7 us -> 12.9 us
  transfers between devices with their start and end apart: 16 -> 58, of which waited for: 7 -> 27; matrix products, arithmetic and copies ran while one was open for 24% -> 36% of each run, Pallas kernels for 0% -> 0%
where the time goes in v1:
time: 521 us; the launch traced here: 516 us
  waiting for transfers between devices  144 us (28%)
  other arithmetic  98.3 us (19%)
  matrix products  89.5 us (17%)
  local copies, waits for them, and re-layouts  86.6 us (17%)
  starting transfers between devices  81.8 us (16%)
  between operations  16.2 us (3%)
    ppermute x46, waiting for transfers between devices, shifted(): return lax.ppermute(cells, axis, pairs)  108 us
    ppermute x46, starting transfers between devices, shifted(): return lax.ppermute(cells, axis, pairs)  57.9 us
    all_gather x1, waiting for transfers between devices, local(): lax.all_gather(w_qkv.astype(jnp.bfloat16), 'dp', axis=0, tiled=True)  22.9 us
    ppermute x4, starting transfers between devices, extended(): lax.ppermute(tail, axis, [(i, (i + 1) % count) for i in range(ends)])  18.6 us
    reshape x5, local copies, waits for them, and re-layouts, local(): near_kv[:, tap_start:tap_start + tok_count]  16.8 us
    convert_element_type x1, other arithmetic, local(): activated_b = activated.astype(jnp.bfloat16)  15.7 us
    unnamed x211, local copies, waits for them, and re-layouts  12.9 us
    slice x5, local copies, waits for them, and re-layouts, local(): near_kv[:, tap_start:tap_start + tok_count]  12.5 us
  transfers between devices with their start and end apart: 58, of which 27 were waited for; matrix products, arithmetic and copies ran while one was open for 36% of the time, Pallas kernels for 0%

profile of v1, /device:TPU:0, one launch (start us, length us, event | category | flops | bytes accessed | tf_op | source)
XLA Modules:
  0.0 516.5 jit_solution(9476595184528420839)
XLA Ops:
  20.8 22.9 %all-gather.5.cloned.1.call-done = bf16[768,2304]{1,0:T(8,128)(2,1)} async-done(((bf16[192,2304]{1,0:T(8,128)(2,1)}), bf16[768,2304]{1,0:T(8,128)(2,1)}) %all-gather.5.cloned.1.call-update) | async-done | bytes 3538960 | tf_op jit(solution)/shard_map/all_gather | solution.py:217
  49.9 5.7 %collective-permute-start = (bf16[2,64,1536]{2,1,0:T(8,128)(2,1)}, bf16[2,64,1536]{2,1,0:T(8,128)(2,1)}, u32[]{:S(2)}, u32[]{:S(2)}) collective-permute-start(bf16[2,64,1536]{2,1,0:T(8,128)(2,1)} %get-tuple-element.103), channel_id=1, source_target_pairs={{0,4},{4,8},{8,12},{12,16},{16,20},{20,24},{24,28},{1,5},{5,9},{9,... | collective-permute-start | bytes 1179656 | tf_op jit(solution)/shard_map/ppermute | solution.py:24
  62.0 8.4 %collective-permute-done = bf16[2,64,1536]{2,1,0:T(8,128)(2,1)} collective-permute-done((bf16[2,64,1536]{2,1,0:T(8,128)(2,1)}, bf16[2,64,1536]{2,1,0:T(8,128)(2,1)}, u32[]{:S(2)}, u32[]{:S(2)}) %collective-permute-start) | collective-permute-done | bytes 393248 | tf_op jit(solution)/shard_map/ppermute | solution.py:24
  100.6 6.4 %fusion.81 = bf16[2,64,1536]{2,0,1:T(2,128)(2,1)} fusion(pred[2,64]{0,1:T(8,128)(4,1)S(1)} %copy.134, pred[2,64]{0,1:T(8,128)(4,1)} %copy.132, pred[2,64]{0,1:T(8,128)(4,1)} %copy.130, pred[2,64]{0,1:T(8,128)(4,1)} %copy.128, pred[2,64]{0,1:T(8,128)(4,1)S(1)} %copy.124, f32[1536]{0:T(1024)} %get-tuple-element.76, f32[1536]{0:T(1024)} %get-tuple-element.73, ...), kind=kLoop, calls=%fused_computation.185 | loop fusion | flops 3932160 | bytes 2390656 | tf_op jit(solution)/shard_map/convert_element_type | solution.py:287
  108.3 5.7 %collective-permute-start.2 = (bf16[2,64,1536]{2,0,1:T(2,128)(2,1)}, bf16[2,64,1536]{2,0,1:T(2,128)(2,1)}, u32[]{:S(2)}, u32[]{:S(2)}) collective-permute-start(bf16[2,64,1536]{2,0,1:T(2,128)(2,1)} %fusion.81), channel_id=1, source_target_pairs={{0,4},{4,8},{8,12},{12,16},{16,20},{20,24},{24,28},{1,5},{5,9},{9,... | collective-permute-start | bytes 1179656 | tf_op jit(solution)/shard_map/ppermute | solution.py:24
  150.2 7.4 %fusion.48 = (u8[256,3072]{1,0:T(8,128)(4,1)S(1)}, u8[256,3072]{1,0:T(8,128)(4,1)S(1)}, f32[2,256,3072]{2,1,0:T(8,128)S(1)}) fusion(f32[3072]{0:T(1024)S(1)} %copy-done.57, bf16[768,3072]{1,0:T(8,128)(2,1)} %all-gather.9.cloned.1.call-done, f32[2,256,768]{2,1,0:T(8,128)} %copy-done.17, f32[768]{0:T(1024)S(1)} %copy-done.75, f32[768]{0:T(1024)S(1)} %copy-done.67, ...), kind=kOutput, calls=%fused_computation.119 | convolution fusion | flops 2438332416 | bytes 14178304 | tf_op jit(solution)/shard_map/rtd,df->rtf/dot_general | solution.py:304
  160.3 15.7 %multiply_convert_fusion.1 = (bf16[2,256,3072]{2,1,0:T(8,128)(2,1)}, f32[2,256,3072]{2,1,0:T(8,128)}) fusion(f32[2,256,3072]{2,1,0:T(8,128)S(1)} %get-tuple-element.162, f32[3072]{0:T(1024)S(1)} %copy-done.57, u8[256,3072]{1,0:T(8,128)(4,1)S(1)} %get-tuple-element.53, u8[256,3072]{1,0:T(8,128)(4,1)S(1)} %get-tuple-element.52), kind=kLoop, calls=%fused_computation.19 | loop fusion | flops 111673344 | bytes 17313792 | tf_op jit(solution)/shard_map/convert_element_type | solution.py:307
  176.0 6.5 %fusion.145 = (f32[2,256]{1,0:T(2,128)S(1)}, f32[2,256,768]{2,1,0:T(8,128)S(1)}) fusion(f32[768]{0:T(1024)S(1)} %copy-done.74, bf16[2,256,3072]{2,1,0:T(8,128)(2,1)} %get-tuple-element.96, bf16[3072,768]{1,0:T(8,128)(2,1)} %all-gather.11.cloned.1.call-done, f32[768]{0:T(1024)S(1)} %copy-done.75, f32[768]{0:T(1024)S(1)} %copy-done.67, ...), kind=kOutput, calls=%fused_computation.366 | convolution fusion | flops 2418671104 | bytes 11025408 | tf_op jit(solution)/shard_map/rtf,fd->rtd/dot_general | solution.py:309
  191.3 9.6 %convert_reduce_fusion = (f32[3072]{0:T(1024)}, bf16[2,256,3072]{2,1,0:T(8,128)(2,1)}) fusion(f32[2,256,3072]{2,1,0:T(8,128)S(1)} %bitcast.378, bf16[2,256,768]{2,1,0:T(8,128)(2,1)} %copy-done.38, bf16[3072,768]{1,0:T(8,128)(2,1)} %all-gather.11.cloned.1.call-done, f32[2,256,3072]{2,1,0:T(8,128)S(1)} %bitcast.376, f32[3072]{0:T(1024)S(1)} %copy-done.57), kind=kOutput, calls=%fused_computation.17 | convolution fusion | flops 2442654720 | bytes 21258240 | tf_op jit(solution)/shard_map/rtd,fd->rtf/dot_general | solution.py:321
  200.9 6.6 %bitcast_convert_fusion.1 = bf16[768,3072]{1,0:T(8,128)(2,1)} fusion(bf16[2,256,3072]{2,1,0:T(8,128)(2,1)} %get-tuple-element.171, f32[2,256,768]{2,1,0:T(8,128)S(1)} %copy-done.18, f32[768]{0:T(1024)S(1)} %copy-done.75, f32[768]{0:T(1024)S(1)} %copy-done.67, f32[2,256]{1,0:T(2,128)S(1)} %add_rsqrt_fusion.1, f32[2,256]{1,0:T(2,128)S(1)} %broadcast_multiply_fusion.5), kind=kOutput, calls=%fused_computation.2 | convolution fusion | flops 2420244480 | bytes 9447424 | tf_op jit(solution)/shard_map/rtd,rtf->df/dot_general | solution.py:325
  207.5 6.4 %multiply_reduce_fusion.2 = (f32[768]{0:T(1024)}, f32[2,256]{1,0:T(2,128)S(1)}, f32[2,256]{1,0:T(2,128)S(1)}, f32[768]{0:T(1024)}, f32[2,256,768]{2,1,0:T(8,128)S(1)}) fusion(f32[2,256,768]{2,1,0:T(8,128)S(1)} %copy-done.18, f32[2,256]{1,0:T(2,128)S(1)} %add_rsqrt_fusion.1, f32[2,256]{1,0:T(2,128)S(1)} %broadcast_multiply_fusion.5, ...), kind=kOutput, calls=%fused_computation.107 | convolution fusion | flops 2422994432 | bytes 13398016 | tf_op jit(solution)/shard_map/rtf,df->rtd/dot_general | solution.py:326
  237.6 6.4 %multiply_reduce_fusion = (f32[2,12,256]{2,1,0:T(8,128)S(1)}, f32[2,12,256,384]{3,2,1,0:T(8,128)}) fusion(f32[2,12,256]{2,1,0:T(8,128)S(1)} %copy-done.41, f32[2,12,256,384]{3,2,1,0:T(8,128)S(1)} %bitcast.360, pred[2,256,384]{2,1,0:T(8,128)(4,1)S(1)} %copy-done.22, bf16[2,256,12,64]{1,3,2,0:T(8,128)(2,1)S(1)} %bitcast.417, ...), kind=kOutput, calls=%fused_computation.4 | convolution fusion | flops 316139520 | bytes 21086208 | tf_op jit(solution)/shard_map/rqhd,rkhd->rhqk/dot_general | solution.py:80
  260.8 5.1 collective-permute-start.4
  267.2 8.3 %multiply_convert_fusion = bf16[2,12,256,384]{3,2,1,0:T(8,128)(2,1)S(1)} fusion(f32[2,12,256,384]{3,2,1,0:T(8,128)} %get-tuple-element.169, f32[2,12,256]{2,1,0:T(8,128)S(1)} %get-tuple-element.168, f32[2,12,256]{2,1,0:T(8,128)S(1)} %copy-done.41, f32[2,12,256,384]{3,2,1,0:T(8,128)} %copy-done, pred[2,256,384]{2,1,0:T(8,128)(4,1)S(1)} %copy-done.22), kind=kLoop, calls=%fused_computation.3 | loop fusion | flops 16515072 | bytes 23838720 | tf_op jit(solution)/shard_map/convert_element_type | solution.py:84
  287.2 11.6 %fusion.77 = (f32[1536]{0:T(1024)S(1)}, f32[1536]{0:T(1024)S(1)}, f32[1536]{0:T(1024)S(1)}, f32[1536]{0:T(1024)S(1)}, f32[1536]{0:T(1024)S(1)}, /*index=5*/f32[2,64,1536]{2,0,1:T(2,128)}) fusion(pred[2,64]{0,1:T(8,128)(4,1)S(1)} %copy.134, bf16[2,64,1,1536]{3,2,1,0:T(2,128)(2,1)S(1)} %copy-done.9, bf16[2,64,1,1536]{3,2,1,0:T(2,128)(2,1)S(1)} %copy-done.10, ...), kind=kLoop, calls=%fused_computation.175 | loop fusion | flops 6087168 | bytes 6716032 | tf_op jit(solution)/shard_map/reduce_sum | solution.py:362
  325.2 5.5 %collective-permute-done.33 = f32[19,768]{1,0:T(8,128)S(1)} collective-permute-done((f32[19,768]{1,0:T(8,128)S(1)}, f32[19,768]{1,0:T(8,128)S(1)}, u32[]{:S(2)}, u32[]{:S(2)}) %collective-permute-start.33) | collective-permute-done | bytes 58400 | tf_op jit(solution)/shard_map/ppermute | solution.py:111
  330.7 5.6 %collective-permute-done.32 = f32[19,768]{1,0:T(8,128)S(1)} collective-permute-done((f32[19,768]{1,0:T(8,128)S(1)}, f32[19,768]{1,0:T(8,128)S(1)}, u32[]{:S(2)}, u32[]{:S(2)}) %collective-permute-start.32) | collective-permute-done | bytes 58400 | tf_op jit(solution)/shard_map/ppermute | solution.py:111
  383.3 16.8 %collective-permute-done.9 = bf16[192,2304]{1,0:T(8,128)(2,1)S(1)} collective-permute-done((bf16[192,2304]{1,0:T(8,128)(2,1)S(1)}, bf16[192,2304]{1,0:T(8,128)(2,1)S(1)}, u32[]{:S(2)}, u32[]{:S(2)}) %collective-permute-start.9) | collective-permute-done | bytes 884768 | tf_op jit(solution)/shard_map/ppermute | solution.py:111
  400.6 9.3 %collective-permute-done.35 = bf16[2,96,3072]{2,1,0:T(8,128)(2,1)S(1)} collective-permute-done((bf16[2,96,3072]{2,1,0:T(8,128)(2,1)S(1)}, bf16[2,96,3072]{2,1,0:T(8,128)(2,1)S(1)}, u32[]{:S(2)}, u32[]{:S(2)}) %collective-permute-start.35) | collective-permute-done | bytes 1179680 | tf_op jit(solution)/shard_map/ppermute | solution.py:111
  419.5 5.8 %collective-permute-done.45 = bf16[768,768]{1,0:T(8,128)(2,1)S(1)} collective-permute-done((bf16[768,768]{1,0:T(8,128)(2,1)S(1)}, bf16[768,768]{1,0:T(8,128)(2,1)S(1)}, u32[]{:S(2)}, u32[]{:S(2)}) %collective-permute-start.45) | collective-permute-done | bytes 1179680 | tf_op jit(solution)/shard_map/ppermute | solution.py:111
  452.2 11.4 %collective-permute-done.38 = bf16[24,3072]{1,0:T(8,128)(2,1)S(1)} collective-permute-done((bf16[24,3072]{1,0:T(8,128)(2,1)S(1)}, bf16[24,3072]{1,0:T(8,128)(2,1)S(1)}, u32[]{:S(2)}, u32[]{:S(2)}) %collective-permute-start.38) | collective-permute-done | bytes 147488 | tf_op jit(solution)/shard_map/ppermute | solution.py:111
  468.1 6.6 %collective-permute-done.48 = bf16[96,768]{1,0:T(8,128)(2,1)S(1)} collective-permute-done((bf16[96,768]{1,0:T(8,128)(2,1)S(1)}, bf16[96,768]{1,0:T(8,128)(2,1)S(1)}, u32[]{:S(2)}, u32[]{:S(2)}) %collective-permute-start.48) | collective-permute-done | bytes 147488 | tf_op jit(solution)/shard_map/ppermute | solution.py:111
  479.9 6.6 %collective-permute-start.50 = (bf16[96,768]{1,0:T(8,128)(2,1)S(1)}, bf16[96,768]{1,0:T(8,128)(2,1)S(1)}, u32[]{:S(2)}, u32[]{:S(2)}) collective-permute-start(bf16[96,768]{1,0:T(8,128)(2,1)S(1)} %get-tuple-element.84), channel_id=1, source_target_pairs={{0,24},{4,28},{8,0},{12,4},{16,8},{20,12},{24,16},{28,20},{1,25},{... | collective-permute-start | bytes 442376 | tf_op jit(solution)/shard_map/ppermute | solution.py:111
  492.8 8.8 %collective-permute-done.43 = bf16[96,3072]{1,0:T(8,128)(2,1)S(1)} collective-permute-done((bf16[96,3072]{1,0:T(8,128)(2,1)S(1)}, bf16[96,3072]{1,0:T(8,128)(2,1)S(1)}, u32[]{:S(2)}, u32[]{:S(2)}) %collective-permute-start.43) | collective-permute-done | bytes 589856 | tf_op jit(solution)/shard_map/ppermute | solution.py:111
  (518 shorter events, 291.2 us)
Async XLA Ops:
  7.2 36.5 %all-gather.5.cloned.1.call-start = ((), (), s32[]{:S(2)}) async-start(), calls=%async_computation | async-start | bytes 4423680 | tf_op jit(solution)/shard_map/all_gather | solution.py:217
  9.9 136.1 %all-gather.7.cloned.1.call-start = ((), (), s32[]{:S(2)}) async-start(), calls=%async_computation.1 | async-start | bytes 1474560 | tf_op jit(solution)/shard_map/all_gather | solution.py:218
  10.7 139.5 %all-gather.9.cloned.1.call-start = ((), (), s32[]{:S(2)}) async-start(), calls=%async_computation.2 | async-start | bytes 5898240 | tf_op jit(solution)/shard_map/all_gather | solution.py:219
  12.0 163.9 %all-gather.11.cloned.1.call-start = ((), (), s32[]{:S(2)}) async-start(), calls=%async_computation.3 | async-start | bytes 5898240 | tf_op jit(solution)/shard_map/all_gather | solution.py:220
  49.9 20.5 %collective-permute-start = (bf16[2,64,1536]{2,1,0:T(8,128)(2,1)}, bf16[2,64,1536]{2,1,0:T(8,128)(2,1)}, u32[]{:S(2)}, u32[]{:S(2)}) collective-permute-start(bf16[2,64,1536]{2,1,0:T(8,128)(2,1)} %get-tuple-element.103), channel_id=1, source_target_pairs={{0,4},{4,8},{8,12},{12,16},{16,20},{20,24},{24,28},{1,5},{5,9},{9,... | collective-permute-start | bytes 1179656 | tf_op jit(solution)/shard_map/ppermute | solution.py:24
  107.0 18.9 %collective-permute-start.3 = (bf16[2,64,1536]{2,0,1:T(2,128)(2,1)}, bf16[2,64,1536]{2,0,1:T(2,128)(2,1)}, u32[]{:S(2)}, u32[]{:S(2)}) collective-permute-start(bf16[2,64,1536]{2,0,1:T(2,128)(2,1)} %fusion.81), channel_id=1, source_target_pairs={{4,0},{8,4},{12,8},{16,12},{20,16},{24,20},{28,24},{5,1},{9,5},{13... | collective-permute-start | bytes 1179656 | tf_op jit(solution)/shard_map/ppermute | solution.py:26
  108.3 21.1 %collective-permute-start.2 = (bf16[2,64,1536]{2,0,1:T(2,128)(2,1)}, bf16[2,64,1536]{2,0,1:T(2,128)(2,1)}, u32[]{:S(2)}, u32[]{:S(2)}) collective-permute-start(bf16[2,64,1536]{2,0,1:T(2,128)(2,1)} %fusion.81), channel_id=1, source_target_pairs={{0,4},{4,8},{8,12},{12,16},{16,20},{20,24},{24,28},{1,5},{5,9},{9,... | collective-permute-start | bytes 1179656 | tf_op jit(solution)/shard_map/ppermute | solution.py:24
  248.4 73.3 %collective-permute-start.18 = (bf16[2,192,768]{2,1,0:T(8,128)(2,1)}, bf16[2,192,768]{2,1,0:T(8,128)(2,1)}, u32[]{:S(2)}, u32[]{:S(2)}) collective-permute-start(bf16[2,192,768]{2,1,0:T(8,128)(2,1)} %dynamic-slice_bitcast_fusion.8), channel_id=1, source_target_pairs={{0,1},{1,0},{2,3},{3,2},{4,5},{5,4},{6,7},{7,6},{8,9},{9,8},{10,11... | collective-permute-start | bytes 1769480 | tf_op jit(solution)/shard_map/ppermute | solution.py:111
  260.8 26.4 %collective-permute-start.4 = (bf16[2,64,1536]{2,0,1:T(2,128)(2,1)}, bf16[2,64,1536]{2,0,1:T(2,128)(2,1)}, u32[]{:S(2)}, u32[]{:S(2)}) collective-permute-start(bf16[2,64,1536]{2,0,1:T(2,128)(2,1)} %get-tuple-element.115), channel_id=1, source_target_pairs={{0,4},{4,8},{8,12},{12,16},{16,20},{20,24},{24,28},{1,5},{5,9},{9,... | collective-permute-start | bytes 1179656 | tf_op jit(solution)/shard_map/ppermute | solution.py:24
  265.9 21.3 %collective-permute-start.5 = (bf16[2,64,1536]{2,0,1:T(2,128)(2,1)}, bf16[2,64,1536]{2,0,1:T(2,128)(2,1)}, u32[]{:S(2)}, u32[]{:S(2)}) collective-permute-start(bf16[2,64,1536]{2,0,1:T(2,128)(2,1)} %get-tuple-element.116), channel_id=1, source_target_pairs={{4,0},{8,4},{12,8},{16,12},{20,16},{24,20},{28,24},{5,1},{9,5},{13... | collective-permute-start | bytes 1179656 | tf_op jit(solution)/shard_map/ppermute | solution.py:26
  312.6 30.7 %collective-permute-start.6 = (bf16[2,64,1536]{2,1,0:T(8,128)(2,1)S(1)}, bf16[2,64,1536]{2,1,0:T(8,128)(2,1)S(1)}, u32[]{:S(2)}, u32[]{:S(2)}) collective-permute-start(bf16[2,64,1536]{2,1,0:T(8,128)(2,1)S(1)} %get-tuple-element.98), channel_id=1, source_target_pairs={{0,4},{4,8},{8,12},{12,16},{16,20},{20,24},{24,28},{1,5},{5,9},{9,... | collective-permute-start | bytes 1179656 | tf_op jit(solution)/shard_map/ppermute | solution.py:24
  314.6 28.6 %collective-permute-start.7 = (bf16[2,64,1536]{2,1,0:T(8,128)(2,1)S(1)}, bf16[2,64,1536]{2,1,0:T(8,128)(2,1)}, u32[]{:S(2)}, u32[]{:S(2)}) collective-permute-start(bf16[2,64,1536]{2,1,0:T(8,128)(2,1)S(1)} %get-tuple-element.99), channel_id=1, source_target_pairs={{4,0},{8,4},{12,8},{16,12},{20,16},{24,20},{28,24},{5,1},{9,5},{13... | collective-permute-start | bytes 1179656 | tf_op jit(solution)/shard_map/ppermute | solution.py:26
  330.6 47.6 %collective-permute-start.34 = (bf16[2,192,3072]{2,1,0:T(8,128)(2,1)}, bf16[2,192,3072]{2,1,0:T(8,128)(2,1)}, u32[]{:S(2)}, u32[]{:S(2)}) collective-permute-start(bf16[2,192,3072]{2,1,0:T(8,128)(2,1)} %dynamic-slice_bitcast_fusion.1), channel_id=1, source_target_pairs={{0,1},{1,0},{2,3},{3,2},{4,5},{5,4},{6,7},{7,6},{8,9},{9,8},{10,11... | collective-permute-start | bytes 7077896 | tf_op jit(solution)/shard_map/ppermute | solution.py:111
  336.3 45.1 %collective-permute-start.44 = (bf16[2,768,768]{2,1,0:T(8,128)(2,1)}, bf16[2,768,768]{2,1,0:T(8,128)(2,1)S(1)}, u32[]{:S(2)}, u32[]{:S(2)}) collective-permute-start(bf16[2,768,768]{2,1,0:T(8,128)(2,1)} %dynamic-slice_bitcast_fusion), channel_id=1, source_target_pairs={{0,1},{1,0},{2,3},{3,2},{4,5},{5,4},{6,7},{7,6},{8,9},{9,8},{10,11... | collective-permute-start | bytes 7077896 | tf_op jit(solution)/shard_map/ppermute | solution.py:111
  377.4 22.7 %collective-permute-start.9 = (bf16[192,2304]{1,0:T(8,128)(2,1)S(1)}, bf16[192,2304]{1,0:T(8,128)(2,1)S(1)}, u32[]{:S(2)}, u32[]{:S(2)}) collective-permute-start(bf16[192,2304]{1,0:T(8,128)(2,1)S(1)} %dynamic-slice_bitcast_fusion.5), channel_id=1, source_target_pairs={{0,2},{1,3},{2,0},{3,1},{4,6},{5,7},{6,4},{7,5},{8,10},{9,11},{10,... | collective-permute-start | bytes 2654216 | tf_op jit(solution)/shard_map/ppermute | solution.py:111
  381.0 29.0 %collective-permute-start.35 = (bf16[2,96,3072]{2,1,0:T(8,128)(2,1)S(1)}, bf16[2,96,3072]{2,1,0:T(8,128)(2,1)S(1)}, u32[]{:S(2)}, u32[]{:S(2)}) collective-permute-start(bf16[2,96,3072]{2,1,0:T(8,128)(2,1)S(1)} %dynamic-slice_bitcast_fusion.4), channel_id=1, source_target_pairs={{0,4},{4,0},{8,12},{12,8},{16,20},{20,16},{24,28},{28,24},{1,5},{5... | collective-permute-start | bytes 3538952 | tf_op jit(solution)/shard_map/ppermute | solution.py:111
  382.0 43.3 %collective-permute-start.45 = (bf16[768,768]{1,0:T(8,128)(2,1)S(1)}, bf16[768,768]{1,0:T(8,128)(2,1)S(1)}, u32[]{:S(2)}, u32[]{:S(2)}) collective-permute-start(bf16[768,768]{1,0:T(8,128)(2,1)S(1)} %dynamic-slice_bitcast_fusion.3), channel_id=1, source_target_pairs={{0,2},{1,3},{2,0},{3,1},{4,6},{5,7},{6,4},{7,5},{8,10},{9,11},{10,... | collective-permute-start | bytes 3538952 | tf_op jit(solution)/shard_map/ppermute | solution.py:111
  410.4 29.1 %collective-permute-start.36 = (bf16[96,3072]{1,0:T(8,128)(2,1)S(1)}, bf16[96,3072]{1,0:T(8,128)(2,1)S(1)}, u32[]{:S(2)}, u32[]{:S(2)}) collective-permute-start(bf16[96,3072]{1,0:T(8,128)(2,1)S(1)} %dynamic-slice_bitcast_fusion.7), channel_id=1, source_target_pairs={{0,2},{1,3},{2,0},{3,1},{4,6},{5,7},{6,4},{7,5},{8,10},{9,11},{10,... | collective-permute-start | bytes 1769480 | tf_op jit(solution)/shard_map/ppermute | solution.py:111
  438.1 53.2 %collective-permute-start.17 = (bf16[96,2304]{1,0:T(8,128)(2,1)S(1)}, bf16[96,2304]{1,0:T(8,128)(2,1)S(1)}, u32[]{:S(2)}, u32[]{:S(2)}) collective-permute-start(bf16[96,2304]{1,0:T(8,128)(2,1)S(1)} %bitcast.406), channel_id=1, source_target_pairs={{0,4},{4,0},{8,12},{12,8},{16,20},{20,16},{24,28},{28,24},{1,5},{5... | collective-permute-start | bytes 1327112 | tf_op jit(solution)/shard_map/ppermute | solution.py:111
  443.6 19.9 %collective-permute-start.38 = (bf16[24,3072]{1,0:T(8,128)(2,1)S(1)}, bf16[24,3072]{1,0:T(8,128)(2,1)S(1)}, u32[]{:S(2)}, u32[]{:S(2)}) collective-permute-start(bf16[24,3072]{1,0:T(8,128)(2,1)S(1)} %get-tuple-element.131), channel_id=1, source_target_pairs={{0,16},{4,20},{8,24},{12,28},{16,0},{20,4},{24,8},{28,12},{1,17},{... | collective-permute-start | bytes 442376 | tf_op jit(solution)/shard_map/ppermute | solution.py:111
  443.8 19.8 %collective-permute-start.47 = (bf16[96,768]{1,0:T(8,128)(2,1)S(1)}, bf16[96,768]{1,0:T(8,128)(2,1)S(1)}, u32[]{:S(2)}, u32[]{:S(2)}) collective-permute-start(bf16[96,768]{1,0:T(8,128)(2,1)S(1)} %get-tuple-element.126), channel_id=1, source_target_pairs={{0,8},{4,12},{8,16},{12,20},{16,24},{20,28},{24,0},{28,4},{1,9},{5... | collective-permute-start | bytes 442376 | tf_op jit(solution)/shard_map/ppermute | solution.py:111
  448.4 19.2 %collective-permute-start.49 = (bf16[96,768]{1,0:T(8,128)(2,1)S(1)}, bf16[96,768]{1,0:T(8,128)(2,1)S(1)}, u32[]{:S(2)}, u32[]{:S(2)}) collective-permute-start(bf16[96,768]{1,0:T(8,128)(2,1)S(1)} %get-tuple-element.127), channel_id=1, source_target_pairs={{0,24},{4,28},{8,0},{12,4},{16,8},{20,12},{24,16},{28,20},{1,25},{... | collective-permute-start | bytes 442376 | tf_op jit(solution)/shard_map/ppermute | solution.py:111
  450.9 23.8 %collective-permute-start.48 = (bf16[96,768]{1,0:T(8,128)(2,1)S(1)}, bf16[96,768]{1,0:T(8,128)(2,1)S(1)}, u32[]{:S(2)}, u32[]{:S(2)}) collective-permute-start(bf16[96,768]{1,0:T(8,128)(2,1)S(1)} %get-tuple-element.128), channel_id=1, source_target_pairs={{0,16},{4,20},{8,24},{12,28},{16,0},{20,4},{24,8},{28,12},{1,17},{... | collective-permute-start | bytes 442376 | tf_op jit(solution)/shard_map/ppermute | solution.py:111
  463.6 22.9 %collective-permute-start.42 = (bf16[24,3072]{1,0:T(8,128)(2,1)S(1)}, bf16[24,3072]{1,0:T(8,128)(2,1)S(1)}, u32[]{:S(2)}, u32[]{:S(2)}) collective-permute-start(bf16[24,3072]{1,0:T(8,128)(2,1)S(1)} %get-tuple-element.86), channel_id=1, source_target_pairs={{0,8},{4,12},{8,16},{12,20},{16,24},{20,28},{24,0},{28,4},{1,9},{5... | collective-permute-start | bytes 442376 | tf_op jit(solution)/shard_map/ppermute | solution.py:111
  (127 other events, 971.5 us)
Sparse Core Ops, SparseCore 0:
  10.2 33.4 all-gather.4
  45.2 17.4 all-gather.6
  64.3 37.4 all-gather.8
  103.3 37.4 all-gather.10

commit v2 on v0

v2 whole, which is shorter than its diff:
```python
from functools import partial

import jax
import jax.numpy as jnp
from jax import lax
from jax.experimental import pallas as pl
from jax.experimental.pallas import tpu as pltpu
from jax.sharding import PartitionSpec as P

HEAD = 64
WIN = 128
PWIN = 512
LANES = 128
GROUP = 256
BLOCK = 128
PAD = 16
F32 = jnp.float32
BF16 = jnp.bfloat16

SMALL_COST = pl.CostEstimate(flops=10**11, bytes_accessed=1, transcendentals=0)

epsilon = 1e-05


def digit_of(axis, stride, radix):
    return (lax.axis_index(axis) // stride) % radix


def shifted(cells, axis, stride, radix, step):
    pairs = []
    for i in range(lax.axis_size(axis)):
        here = (i // stride) % radix
        pairs.append((i, i + ((here + step) % radix - here) * stride))
    return lax.ppermute(cells, axis, pairs)


def moved(cells, step):
    count = lax.axis_size("seq")
    pairs = [(i, i + step) for i in range(count) if 0 <= i + step < count]
    return lax.ppermute(cells, "seq", pairs)


def after(cells, *earlier):
    return lax.optimization_barrier((cells, *earlier))[0]


def gathered(shard):
    return shard, shifted(shard, "dp", 1, 2, 1), shifted(shard, "dp", 2, 2, 1)


def with_last(pieces, *earlier):
    partner = after(pieces[2], *earlier) if earlier else pieces[2]
    return *pieces, shifted(partner, "dp", 1, 2, 1)


def piece_owners():
    mine = lax.axis_index("dp")
    turn = 1 - 2 * lax.rem(mine, 2)
    partner = lax.rem(mine + 2, 4)
    return mine, mine + turn, partner, partner + turn


class Order:
    def __init__(self, last):
        self.last = last

    def __call__(self, step, cells, *rest, **options):
        out = step(after(cells, self.last), *rest, **options)
        self.last = out[0]
        return out


def bit_of(name):
    if name in "cy":
        return "dp", 1 << "cy".index(name)
    return "seq", 1 << "xlhijk".index(name)


def mine_of(name):
    return digit_of(*bit_of(name), 2)


def swapped(cells, name):
    axis, stride = bit_of(name)
    return shifted(cells, axis, stride, 2, 1)


def added(kept, received):
    return (kept.astype(F32) + received.astype(F32)).astype(BF16)


def split(kept, received, dim, name):
    mine = mine_of(name)

    def part(index):
        return added(
            lax.dynamic_index_in_dim(kept, index, dim, keepdims=False),
            lax.dynamic_index_in_dim(received, index, dim, keepdims=False),
        )

    return part(1 - mine), part(mine)


def summed(kept, received):
    return (added(kept, received),)


def joined(own, received, dim, name, dtype=BF16):
    first = mine_of(name) == 0
    cells = jnp.stack(
        [jnp.where(first, own, received), jnp.where(first, received, own)], axis=dim
    )
    return (cells.astype(dtype),)


def input_sum_kernel(own, left, right, last, out):
    tokens = own.shape[1]
    out[...] = own[...] + left[...].astype(F32) + right[...].astype(F32)
    out[:, tokens - PAD :] += last[...].astype(F32)


def input_sum(own, left, right, last):
    rows, tokens, width = own.shape
    block = pl.BlockSpec((1, tokens, width), lambda i: (i, 0, 0))
    return pl.pallas_call(
        input_sum_kernel,
        grid=(rows,),
        in_specs=[block] * 3 + [pl.BlockSpec((1, PAD, width), lambda i: (i, 0, 0))],
        out_specs=[block],
        out_shape=[jax.ShapeDtypeStruct(own.shape, F32)],
        compiler_params=pltpu.CompilerParams(vmem_limit_bytes=60 * 2**20),
        cost_estimate=SMALL_COST,
        name="input_sum",
    )(own, left, right, last)


def dot_nn(a, b):
    return jnp.dot(a, b, preferred_element_type=F32)


def dot_nt(a, b):
    return lax.dot_general(a, b, (((1,), (1,)), ((), ())), preferred_element_type=F32)


def dot_tn(a, b):
    return lax.dot_general(a, b, (((0,), (0,)), ((), ())), preferred_element_type=F32)


def segment_of(place, starts, lengths, seq_len):
    started = jnp.zeros(place.shape, jnp.int32)
    inside = jnp.zeros(place.shape, jnp.int32)
    for start, length in zip(starts, lengths):
        begun = place >= start
        started = started + jnp.where(begun, 1, 0)
        inside = inside + jnp.where(begun & (place < start + length), 1, 0)
    return jnp.where((place >= 0) & (place < seq_len), 2 * started + 1 - inside, -1)


def iota_of(shape, dim):
    return lax.broadcasted_iota(jnp.int32, shape, dim)


def allowed_bias(q_place, k_place, segment, reach):
    gap = k_place - q_place
    allowed = (segment(q_place) == segment(k_place)) & (gap >= -reach) & (gap < reach)
    return jnp.where(allowed, 0.0, -1e30)


def head_pair(block):
    first = iota_of(block.shape, 1) < HEAD
    zero = jnp.zeros(block.shape, block.dtype)
    return jnp.concatenate([jnp.where(first, block, zero), jnp.where(first, zero, block)], axis=0)


def join_pair(pair):
    rows = pair.shape[0] // 2
    first = iota_of((rows, LANES), 1) < HEAD
    return jnp.where(first, pair[:rows], pair[rows:])


def relative_rows(index, rows):
    core = lax.rem(lax.axis_index("dp"), 2)
    same = 1 - (core + index % 2 - 2 * core * (index % 2))
    return pl.ds(pl.multiple_of((2 * same + index // 2) * rows, 16), rows)


def row_docs(starts_ref, lengths_ref, row, slots):
    return (
        [starts_ref[row, j] for j in range(slots)],
        [lengths_ref[row, j] for j in range(slots)],
    )


def copy_all(copies):
    for copy in copies:
        copy.start()
    for copy in copies:
        copy.wait()


def token_copies(pieces, scratch, sems, rows, tokens):
    copies = []
    extent = PAD + 3 * tokens
    firsts = (0, PAD, PAD + tokens, PAD + 2 * tokens)
    for row in range(rows):
        for k, (piece, first) in enumerate(zip(pieces, firsts)):
            count = PAD if k == 0 else tokens
            copies.append(
                pltpu.make_async_copy(
                    piece.at[row],
                    scratch.at[pl.ds(row * extent + first, count)],
                    sems.at[row * 4 + k],
                )
            )
    return copies


def weight_copies(pieces, scratch, sems, rows):
    return [
        pltpu.make_async_copy(
            piece, scratch.at[pl.ds(pl.multiple_of(index * rows, 16), rows)], sems.at[k]
        )
        for k, (piece, index) in enumerate(zip(pieces, piece_owners()))
    ]


def tap_mask(row, tap, reach, pooled, tokens, starts_ref, lengths_ref, slots, seq_len):
    anchor = lax.axis_index("seq") * tokens
    center = anchor - 4 * reach + 4 * iota_of((pooled, LANES), 0)
    segment = partial(
        segment_of,
        seq_len=seq_len,
        **dict(zip(("starts", "lengths"), row_docs(starts_ref, lengths_ref, row, slots))),
    )
    return jnp.where(segment(center + (tap - 2)) == segment(center), 1.0, 0.0)


def forward_kernel(
    sizes,
    starts_ref,
    lengths_ref,
    x_ll,
    x_l,
    x_own,
    x_r,
    w0,
    w1,
    w2,
    w3,
    pool_ref,
    q_out,
    k_out,
    v_out,
    pk_out,
    pv_out,
    att_out,
    xs,
    ws,
    flat,
    near_bias,
    far_bias,
    taps_ok,
    x_sems,
    w_sems,
):
    rows, tokens, width, seq_len, slots = sizes
    step = pl.program_id(0)
    extent = PAD + 3 * tokens
    half_win = WIN // 2
    reach = PWIN // 8
    pooled = tokens // 4 + 2 * reach
    blocks = tokens // BLOCK
    span = BLOCK + 2 * half_win
    anchor = lax.axis_index("seq") * tokens

    @pl.when(step == 0)
    def _():
        copies = token_copies((x_ll, x_l, x_own, x_r), xs, x_sems, rows, tokens)
        copies += weight_copies((w0, w1, w2, w3), ws, w_sems, width // 4)
        for copy in copies:
            copy.start()
        for row in range(rows):
            starts, lengths = row_docs(starts_ref, lengths_ref, row, slots)
            segment = partial(segment_of, starts=starts, lengths=lengths, seq_len=seq_len)
            for block in range(blocks):
                q_place = anchor + block * BLOCK + iota_of((BLOCK, 1), 0)
                near_place = anchor + block * BLOCK - half_win + iota_of((1, span), 1)
                far_place = anchor - 4 * reach + 4 * iota_of((1, pooled), 1)
                near_bias[row, block] = allowed_bias(q_place, near_place, segment, half_win)
                far_bias[row, block] = allowed_bias(q_place, far_place, segment, 4 * reach)
            for tap in range(5):
                taps_ok[row, tap] = tap_mask(
                    row, tap, reach, pooled, tokens, starts_ref, lengths_ref, slots, seq_len
                )
        for copy in copies:
            copy.wait()

    def columns(part):
        return pl.ds(pl.multiple_of(part * width + step * GROUP, LANES), GROUP)

    x_all = xs[...]
    for row in range(rows):
        own = xs[pl.ds(row * extent + PAD + tokens, tokens)]
        q_out[row] = dot_nn(own, ws[:, columns(0)]).astype(BF16)
    for part, out, pooled_out in ((1, k_out, pk_out), (2, v_out, pv_out)):
        cells = dot_nn(x_all, ws[:, columns(part)]).astype(BF16)
        out[...] = cells.reshape(rows, extent, GROUP)
        for half in range(GROUP // LANES):
            lanes = pl.ds(half * LANES, LANES)
            flat[half] = cells[:, half * LANES : (half + 1) * LANES].astype(F32)
            for row in range(rows):
                total = jnp.zeros((pooled, LANES), F32)
                for tap in range(5):
                    first = row * extent + PAD - 2 + tap
                    tap_rows = flat[half, pl.ds(first, pooled, stride=4)]
                    total = total + tap_rows * taps_ok[row, tap] * pool_ref[part - 1, tap, lanes]
                pooled_out[row, :, lanes] = total.astype(BF16)
    for row in range(rows):
        for half in range(GROUP // LANES):
            lanes = pl.ds(half * LANES, LANES)
            for block in range(blocks):
                queries = q_out[row, pl.ds(block * BLOCK, BLOCK), lanes] * 0.125
                window = pl.ds(PAD + tokens + block * BLOCK - half_win, span)
                keys = jnp.concatenate([k_out[row, window, lanes], pk_out[row, :, lanes]], axis=0)
                values = jnp.concatenate([v_out[row, window, lanes], pv_out[row, :, lanes]], axis=0)
                scores = dot_nt(head_pair(queries.astype(BF16)), keys)
                scores = scores.reshape(2, BLOCK, span + pooled)
                shares = []
                for part, bias in (
                    (scores[..., :span], near_bias[row, block]),
                    (scores[..., span:], far_bias[row, block]),
                ):
                    part = part + bias
                    exponent = jnp.exp(part - jnp.max(part, axis=-1, keepdims=True))
                    normalizer = jnp.sum(exponent, axis=-1, keepdims=True)
                    shares.append((exponent * (1.0 / normalizer)).astype(BF16))
                shares = jnp.concatenate(shares, axis=-1).reshape(2 * BLOCK, span + pooled)
                result = join_pair(dot_nn(shares, values))
                att_out[row, pl.ds(block * BLOCK, BLOCK), lanes] = result.astype(BF16)


def whole(memory_space):
    return pl.BlockSpec(memory_space=memory_space)


def group_block(*lead):
    zeros = (0,) * len(lead)
    return pl.BlockSpec(lead + (GROUP,), lambda g: zeros + (g,))


def attention_forward(starts, lengths, tokens_in, w_pieces, pool_kernel, seq_len):
    rows, tokens, width = tokens_in[2].shape
    extent = PAD + 3 * tokens
    pooled = tokens // 4 + PWIN // 4
    blocks = tokens // BLOCK
    span = BLOCK + WIN
    slots = starts.shape[1]
    return pl.pallas_call(
        partial(forward_kernel, (rows, tokens, width, seq_len, slots)),
        grid=(width // GROUP,),
        in_specs=[whole(pltpu.SMEM)] * 2 + [whole(pl.ANY)] * 8 + [group_block(2, 5)],
        out_specs=[
            group_block(rows, tokens),
            group_block(rows, extent),
            group_block(rows, extent),
            group_block(rows, pooled),
            group_block(rows, pooled),
            group_block(rows, tokens),
        ],
        out_shape=[
            jax.ShapeDtypeStruct((rows, count, width), BF16)
            for count in (tokens, extent, extent, pooled, pooled, tokens)
        ],
        scratch_shapes=[
            pltpu.VMEM((rows * extent, width), BF16),
            pltpu.VMEM((width, 3 * width), BF16),
            pltpu.VMEM((GROUP // LANES, rows * extent, LANES), F32),
            pltpu.VMEM((rows, blocks, BLOCK, span), F32),
            pltpu.VMEM((rows, blocks, BLOCK, pooled), F32),
            pltpu.VMEM((rows, 5, pooled, LANES), F32),
            pltpu.SemaphoreType.DMA((4 * rows,)),
            pltpu.SemaphoreType.DMA((4,)),
        ],
        compiler_params=pltpu.CompilerParams(vmem_limit_bytes=60 * 2**20),
        cost_estimate=SMALL_COST,
        name="attention_forward",
    )(starts, lengths, *tokens_in, *w_pieces, pool_kernel)


def backward_kernel(
    sizes,
    starts_ref,
    lengths_ref,
    x_ll,
    x_l,
    x_own,
    x_r,
    pool_ref,
    q_ref,
    k_ref,
    v_ref,
    pk_ref,
    pv_ref,
    grad_ref,
    dw_sent_in,
    dw_kept_in,
    dw_sent,
    dw_kept,
    dpool_out,
    dq_out,
    dkv_out,
    xs,
    x_turned,
    own_turned,
    flat,
    grad_flat,
    grad_pooled,
    near_bias,
    far_bias,
    taps_ok,
    dw,
    x_sems,
    dw_sems,
):
    first_group, rows, tokens, width, seq_len, slots = sizes
    quarter = width // 4
    step = pl.program_id(0)
    extent = PAD + 3 * tokens
    half_win = WIN // 2
    reach = PWIN // 8
    pooled = tokens // 4 + 2 * reach
    blocks = tokens // BLOCK
    span = BLOCK + 2 * half_win
    anchor = lax.axis_index("seq") * tokens

    @pl.when(step == 0)
    def _():
        copies = token_copies((x_ll, x_l, x_own, x_r), xs, x_sems, rows, tokens)
        for copy in copies:
            copy.start()
        for row in range(rows):
            starts, lengths = row_docs(starts_ref, lengths_ref, row, slots)
            segment = partial(segment_of, starts=starts, lengths=lengths, seq_len=seq_len)
            for block in range(blocks):
                q_place = anchor + block * BLOCK + iota_of((1, BLOCK), 1)
                near_place = anchor + block * BLOCK - half_win + iota_of((span, 1), 0)
                far_place = anchor - 4 * reach + 4 * iota_of((pooled, 1), 0)
                near = allowed_bias(q_place, near_place, segment, half_win)
                far = allowed_bias(q_place, far_place, segment, 4 * reach)
                near_bias[row, block] = jnp.concatenate([near, near], axis=1)
                far_bias[row, block] = jnp.concatenate([far, far], axis=1)
            for tap in range(5):
                taps_ok[row, tap] = tap_mask(
                    row, tap, reach, pooled, tokens, starts_ref, lengths_ref, slots, seq_len
                )
        for copy in copies:
            copy.wait()
        for index in range(4):
            features = pl.ds(index * quarter, quarter)
            place = relative_rows(index, quarter)
            x_turned[place] = xs[:, features].T
            for row in range(rows):
                own_turned[place, pl.ds(row * tokens, tokens)] = xs[
                    pl.ds(row * extent + PAD + tokens, tokens), features
                ].T

    grad_flat[...] = jnp.zeros(grad_flat.shape, F32)
    grad_pooled[...] = jnp.zeros(grad_pooled.shape, F32)
    for row in range(rows):
        for half in range(GROUP // LANES):
            lanes = pl.ds(half * LANES, LANES)
            for block in range(blocks):
                queries = q_ref[row, pl.ds(block * BLOCK, BLOCK), lanes] * 0.125
                queries = head_pair(queries.astype(BF16))
                grads = head_pair(grad_ref[row, pl.ds(block * BLOCK, BLOCK), lanes])
                window_first = PAD + tokens + block * BLOCK - half_win
                window = pl.ds(window_first, span)
                keys = jnp.concatenate([k_ref[row, window, lanes], pk_ref[row, :, lanes]], axis=0)
                values = jnp.concatenate([v_ref[row, window, lanes], pv_ref[row, :, lanes]], axis=0)
                scores = dot_nt(keys, queries)
                grad_shares = dot_nt(values, grads)
                shares_b = []
                grad_scores = []
                for part, bias, grad_part in (
                    (scores[:span], near_bias[row, block], grad_shares[:span]),
                    (scores[span:], far_bias[row, block], grad_shares[span:]),
                ):
                    part = part + bias
                    exponent = jnp.exp(part - jnp.max(part, axis=0, keepdims=True))
                    shares = exponent * (1.0 / jnp.sum(exponent, axis=0, keepdims=True))
                    inner = jnp.sum(shares * grad_part, axis=0, keepdims=True)
                    shares_b.append(shares.astype(BF16))
                    grad_scores.append((shares * (grad_part - inner)).astype(BF16))
                shares_b = jnp.concatenate(shares_b, axis=0)
                grad_scores = jnp.concatenate(grad_scores, axis=0)
                grad_queries = join_pair(dot_tn(grad_scores, keys)) * 0.125
                dq_out[pl.ds(row * tokens + block * BLOCK, BLOCK), lanes] = grad_queries.astype(
                    BF16
                )
                for index, grad_rows in (
                    (0, dot_nn(grad_scores, queries)),
                    (1, dot_nn(shares_b, grads)),
                ):
                    near_rows = pl.ds(row * extent + window_first, span)
                    grad_flat[index, half, near_rows] += grad_rows[:span]
                    far_rows = pl.ds(row * pooled, pooled)
                    grad_pooled[index, far_rows, lanes] += grad_rows[span:]

    for index, cells in ((0, k_ref), (1, v_ref)):
        for half in range(GROUP // LANES):
            lanes = pl.ds(half * LANES, LANES)
            flat[...] = cells[:, :, lanes].reshape(rows * extent, LANES).astype(F32)
            for tap in range(5):
                total = jnp.zeros((1, LANES), F32)
                for row in range(rows):
                    places = pl.ds(row * extent + PAD - 2 + tap, pooled, stride=4)
                    grads = grad_pooled[index, pl.ds(row * pooled, pooled), lanes]
                    grads = grads * taps_ok[row, tap]
                    total = total + jnp.sum(grads * flat[places], axis=0, keepdims=True)
                    grad_flat[index, half, places] = (
                        grad_flat[index, half, places] + grads * pool_ref[index, tap, lanes]
                    )
                dpool_out[index, pl.ds(tap, 1), lanes] = total

    slot = lax.rem(step, 2)

    def dw_copies(slot, group):
        columns = pl.ds(pl.multiple_of(group * GROUP, LANES), GROUP)
        return [
            pltpu.make_async_copy(
                dw.at[slot, k], out.at[:, pl.ds(0, 3), :, columns], dw_sems.at[slot, k]
            )
            for k, out in enumerate((dw_sent, dw_kept))
        ]

    @pl.when(step >= 2)
    def _():
        for copy in dw_copies(slot, first_group + step - 2):
            copy.wait()

    def put(index, cells):
        dw[slot, :, :, index] = cells.astype(BF16).reshape(2, 2, quarter, GROUP)

    put(0, dot_nn(own_turned[...], dq_out[...]))
    for index in range(2):
        cells = jnp.concatenate(
            [grad_flat[index, half] for half in range(GROUP // LANES)], axis=1
        ).astype(BF16)
        dkv_out[index] = cells
        put(1 + index, dot_nn(x_turned[...], cells))
    for copy in dw_copies(slot, first_group + step):
        copy.start()

    @pl.when(step == pl.num_programs(0) - 1)
    def _():
        for copy in dw_copies(slot, first_group + step):
            copy.wait()

    @pl.when((step == pl.num_programs(0) - 1) & (step >= 1))
    def _():
        for copy in dw_copies(1 - slot, first_group + step - 1):
            copy.wait()


def attention_backward(
    grad_att, dw_sent, dw_kept, starts, lengths, tokens_in, pool_kernel, saved, seq_len, groups
):
    rows, tokens, width = tokens_in[2].shape
    extent = PAD + 3 * tokens
    pooled = tokens // 4 + PWIN // 4
    blocks = tokens // BLOCK
    span = BLOCK + WIN
    slots = starts.shape[1]
    quarter = width // 4
    first, count = groups
    columns = count * GROUP

    def read(*lead):
        zeros = (0,) * len(lead)
        return pl.BlockSpec(lead + (GROUP,), lambda g: zeros + (g + first,))

    return pl.pallas_call(
        partial(backward_kernel, (first, rows, tokens, width, seq_len, slots)),
        grid=(count,),
        in_specs=[whole(pltpu.SMEM)] * 2
        + [whole(pl.ANY)] * 4
        + [read(2, 5)]
        + [read(rows, size) for size in (tokens, extent, extent, pooled, pooled, tokens)]
        + [whole(pl.ANY)] * 2,
        out_specs=[
            whole(pl.ANY),
            whole(pl.ANY),
            group_block(2, 5),
            group_block(rows * tokens),
            group_block(2, rows * extent),
        ],
        out_shape=[
            jax.ShapeDtypeStruct(dw_sent.shape, BF16),
            jax.ShapeDtypeStruct(dw_kept.shape, BF16),
            jax.ShapeDtypeStruct((2, 5, columns), F32),
            jax.ShapeDtypeStruct((rows * tokens, columns), BF16),
            jax.ShapeDtypeStruct((2, rows * extent, columns), BF16),
        ],
        scratch_shapes=[
            pltpu.VMEM((rows * extent, width), BF16),
            pltpu.VMEM((width, rows * extent), BF16),
            pltpu.VMEM((width, rows * tokens), BF16),
            pltpu.VMEM((rows * extent, LANES), F32),
            pltpu.VMEM((2, GROUP // LANES, rows * extent, LANES), F32),
            pltpu.VMEM((2, rows * pooled, GROUP), F32),
            pltpu.VMEM((rows, blocks, span, 2 * BLOCK), F32),
            pltpu.VMEM((rows, blocks, pooled, 2 * BLOCK), F32),
            pltpu.VMEM((rows, 5, pooled, LANES), F32),
            pltpu.VMEM((2, 2, 2, 3, quarter, GROUP), BF16),
            pltpu.SemaphoreType.DMA((4 * rows,)),
            pltpu.SemaphoreType.DMA((2, 2)),
        ],
        input_output_aliases={13: 0, 14: 1},
        compiler_params=pltpu.CompilerParams(vmem_limit_bytes=60 * 2**20),
        cost_estimate=SMALL_COST,
        name="attention_backward",
    )(starts, lengths, *tokens_in, pool_kernel, *saved, grad_att, dw_sent, dw_kept)


def input_kernel(sizes, w0, w1, w2, w3, *refs):
    parts, rows, tokens, width = sizes
    grad_q = refs[:parts]
    grad_kv = refs[parts : 2 * parts]
    sum1_ref, dx_own, dx_ll, dx_l, dx_r, ws, sems = refs[2 * parts :]
    extent = PAD + 3 * tokens
    copy_all(weight_copies((w0, w1, w2, w3), ws, sems, width // 4))

    def term(row, first, count, with_queries):
        total = None
        column = 0
        for queries, keyvals in zip(grad_q, grad_kv):
            size = queries.shape[1]
            places = pl.ds(row * extent + first, count)
            terms = [
                (keyvals[index, places], ws[:, pl.ds((1 + index) * width + column, size)])
                for index in range(2)
            ]
            if with_queries:
                terms.append((queries[pl.ds(row * tokens, tokens)], ws[:, pl.ds(column, size)]))
            for grads, weights in terms:
                part = dot_nt(grads, weights)
                total = part if total is None else total + part
            column += size
        return total

    for row in range(rows):
        ahead = term(row, 0, PAD + tokens, False).astype(BF16)
        dx_ll[row] = ahead[:PAD]
        dx_l[row] = ahead[PAD:]
        dx_own[row] = term(row, PAD + tokens, tokens, True) + sum1_ref[row]
        dx_r[row] = term(row, PAD + 2 * tokens, tokens, False).astype(BF16)


def input_gradient(grad_sum1, w_pieces, grad_q, grad_kv):
    rows, tokens, width = grad_sum1.shape
    return pl.pallas_call(
        partial(input_kernel, (len(grad_q), rows, tokens, width)),
        in_specs=[whole(pl.ANY)] * 4 + [whole(pltpu.VMEM)] * (2 * len(grad_q) + 1),
        out_specs=[whole(pltpu.VMEM)] * 4,
        out_shape=[
            jax.ShapeDtypeStruct((rows, tokens, width), F32),
            jax.ShapeDtypeStruct((rows, PAD, width), BF16),
            jax.ShapeDtypeStruct((rows, tokens, width), BF16),
            jax.ShapeDtypeStruct((rows, tokens, width), BF16),
        ],
        scratch_shapes=[pltpu.VMEM((width, 3 * width), BF16), pltpu.SemaphoreType.DMA((4,))],
        compiler_params=pltpu.CompilerParams(vmem_limit_bytes=60 * 2**20),
        cost_estimate=SMALL_COST,
        name="input_gradient",
    )(*w_pieces, *grad_q, *grad_kv, grad_sum1)


def normalized(values):
    centered = values - jnp.mean(values, axis=-1, keepdims=True)
    scale = lax.rsqrt(jnp.mean(centered * centered, axis=-1, keepdims=True) + epsilon)
    return centered * scale, scale


def norm_back(grad_unit, unit, scale):
    return scale * (
        grad_unit
        - jnp.mean(grad_unit, axis=-1, keepdims=True)
        - unit * jnp.mean(grad_unit * unit, axis=-1, keepdims=True)
    )


def column_sum(cells):
    return jnp.sum(cells, axis=0, keepdims=True)


def token_kernel(
    att_ref,
    x_ref,
    cot_ref,
    w0,
    w1,
    w2,
    w3,
    gain1_ref,
    bias1_ref,
    up_bias_ref,
    down_bias_ref,
    gain2_ref,
    bias2_ref,
    out_ref,
    grad_att_out,
    sum1_out,
    down_sent,
    down_kept,
    up_sent,
    up_kept,
    qkv_sent,
    qkv_kept,
    smalls_out,
    w_out,
    w_up,
    w_down,
    unit1,
    scale1,
    normed_b,
    act,
    slope,
    second,
    turned,
    dw_down,
    dw_up,
    dw_out,
    sems,
    dw_sems,
):
    width = att_ref.shape[1]
    count = w_up.shape[0]
    quarter = width // 4
    core = lax.rem(lax.axis_index("dp"), 2)

    def turn(cells):
        for index in range(4):
            turned[relative_rows(index, quarter)] = cells[:, pl.ds(index * quarter, quarter)].T

    out_copies = []

    def send(source, target):
        copy = pltpu.make_async_copy(source, target, dw_sems.at[len(out_copies)])
        copy.start()
        out_copies.append(copy)

    copies = []
    for piece, index in zip((w0, w1, w2, w3), piece_owners()):
        for column in range(1 + count + 4):
            if column == 0:
                target, base = w_out, index * quarter
            elif column <= count:
                target, base = w_up.at[column - 1], index * quarter
            else:
                target, base = w_down.at[index], (column - 1 - count) * quarter
            copies.append(
                pltpu.make_async_copy(
                    piece.at[:, pl.ds(column * width, width)],
                    target.at[pl.ds(pl.multiple_of(base, 16), quarter)],
                    sems.at[len(copies)],
                )
            )
    copy_all(copies)

    first_sum = x_ref[...].astype(F32) + dot_nn(att_ref[...], w_out[...])
    unit, scale = normalized(first_sum)
    unit1[...] = unit
    scale1[...] = scale
    normed = unit * gain1_ref[...] + bias1_ref[...]
    normed_b[...] = normed.astype(BF16)
    second[...] = normed + down_bias_ref[...]
    for block in range(count):
        pre = dot_nn(normed_b[...], w_up[block]) + up_bias_ref[pl.ds(block, 1)]
        below = 0.5 * (1.0 + lax.erf(pre * (0.5**0.5)))
        act[block] = (pre * below).astype(BF16)
        slope[block] = below + pre * jnp.exp(-0.5 * pre * pre) * 0.3989422804014327
        second[...] += dot_nn(act[block], w_down[block])

    unit, scale = normalized(second[...])
    out_ref[...] = unit * gain2_ref[...] + bias2_ref[...]
    cot = cot_ref[...].astype(F32)
    smalls_out[pl.ds(3, 1)] = column_sum(cot * unit)
    smalls_out[pl.ds(4, 1)] = column_sum(cot)
    grad_sum2 = norm_back(cot * gain2_ref[...], unit, scale)
    second[...] = grad_sum2
    grad_second = grad_sum2.astype(BF16)
    smalls_out[pl.ds(2, 1)] = column_sum(grad_second.astype(F32))
    turn(normed_b)
    for y in range(2):
        for same, target in ((0, down_sent), (1, down_kept)):
            block = 2 * y + same * core + (1 - same) * (1 - core)
            dw_down[same, y] = dot_tn(act[block], grad_second).astype(BF16)
            send(dw_down.at[same, y], target.at[y])
    for block in range(count):
        grad_pre = (dot_nt(grad_second, w_down[block]) * slope[block]).astype(BF16)
        smalls_out[pl.ds(5 + block, 1)] = column_sum(grad_pre.astype(F32))
        dw_up[block] = dot_nn(turned[...], grad_pre).astype(BF16)
        for same, target in ((0, up_sent), (1, up_kept)):
            for y in range(2):
                send(
                    dw_up.at[block, pl.ds((2 * same + y) * quarter, quarter)],
                    target.at[y, pl.ds(block * quarter, quarter)],
                )
        second[...] += dot_nt(grad_pre, w_up[block])

    grad_normed = second[...]
    unit = unit1[...]
    smalls_out[pl.ds(0, 1)] = column_sum(grad_normed * unit)
    smalls_out[pl.ds(1, 1)] = column_sum(grad_normed)
    grad_sum1 = norm_back(grad_normed * gain1_ref[...], unit, scale1[...])
    sum1_out[...] = grad_sum1
    grad_branch = grad_sum1.astype(BF16)
    turn(att_ref)
    dw_out[...] = dot_nn(turned[...], grad_branch).astype(BF16)
    for same, target in ((0, qkv_sent), (1, qkv_kept)):
        for y in range(2):
            send(dw_out.at[pl.ds((2 * same + y) * quarter, quarter)], target.at[y, 3])
    grad_att_out[...] = dot_nt(grad_branch, w_out[...]).astype(BF16)
    for copy in out_copies:
        copy.wait()


def token_part(attended, hidden_in, cotangent, w_pieces, vectors):
    rows, tokens, width = hidden_in.shape
    total = rows * tokens
    gain1, bias1, up_bias, down_bias, gain2, bias2 = vectors
    hidden = up_bias.shape[0]
    count = hidden // width
    return pl.pallas_call(
        token_kernel,
        in_specs=[whole(pltpu.VMEM)] * 3 + [whole(pl.ANY)] * 4 + [whole(pltpu.VMEM)] * 6,
        out_specs=[whole(pltpu.VMEM)] * 3 + [whole(pl.ANY)] * 6 + [whole(pltpu.VMEM)],
        out_shape=[
            jax.ShapeDtypeStruct((total, width), F32),
            jax.ShapeDtypeStruct((total, width), BF16),
            jax.ShapeDtypeStruct((total, width), F32),
        ]
        + [jax.ShapeDtypeStruct((2, width, width), BF16)] * 4
        + [jax.ShapeDtypeStruct((2, 4, width // 4, width), BF16)] * 2
        + [jax.ShapeDtypeStruct((5 + count, width), F32)],
        scratch_shapes=[
            pltpu.VMEM((width, width), BF16),
            pltpu.VMEM((count, width, width), BF16),
            pltpu.VMEM((count, width, width), BF16),
            pltpu.VMEM((total, width), F32),
            pltpu.VMEM((total, 1), F32),
            pltpu.VMEM((total, width), BF16),
            pltpu.VMEM((count, total, width), BF16),
            pltpu.VMEM((count, total, width), F32),
            pltpu.VMEM((total, width), F32),
            pltpu.VMEM((width, total), BF16),
            pltpu.VMEM((2, 2, width, width), BF16),
            pltpu.VMEM((count, width, width), BF16),
            pltpu.VMEM((width, width), BF16),
            pltpu.SemaphoreType.DMA((4 * (5 + count),)),
            pltpu.SemaphoreType.DMA((8 + 4 * count,)),
        ],
        compiler_params=pltpu.CompilerParams(vmem_limit_bytes=60 * 2**20),
        cost_estimate=SMALL_COST,
        name="token_part",
    )(
        attended.reshape(total, width),
        hidden_in.reshape(total, width),
        cotangent.reshape(total, width),
        *w_pieces,
        gain1.reshape(1, width),
        bias1.reshape(1, width),
        up_bias.reshape(count, width),
        down_bias.reshape(1, width),
        gain2.reshape(1, width),
        bias2.reshape(1, width),
    )


def local(
    hidden_in,
    cotangent,
    w_qkv,
    w_out,
    pool_kernel,
    norm1_gain,
    norm1_bias,
    w_up,
    up_bias,
    w_down,
    down_bias,
    norm2_gain,
    norm2_bias,
    doc_lengths,
    doc_offsets,
):
    rows, tokens, width = hidden_in.shape
    quarter = width // 4
    hidden = up_bias.shape[0]
    seq_len = tokens * lax.axis_size("seq")
    tokens_in = (
        moved(hidden_in[:, tokens - PAD :], 2),
        moved(hidden_in, 1),
        hidden_in,
    )
    qkv_pieces = with_last(gathered(w_qkv.astype(BF16)))
    tokens_in += (moved(after(hidden_in, tokens_in[1]), -1),)
    rest = jnp.concatenate(
        [w_out, w_up, w_down.reshape(4, quarter, width).transpose(1, 0, 2).reshape(quarter, hidden)],
        axis=1,
    )
    rest_pieces = gathered(
        after(rest.astype(BF16), qkv_pieces[2], tokens_in[1])
    )
    *saved, attended = attention_forward(
        doc_offsets, doc_lengths, tokens_in, qkv_pieces, pool_kernel, seq_len
    )
    rest_pieces = with_last(rest_pieces, attended)
    block_out, grad_att, grad_sum1, *terms, smalls = token_part(
        attended,
        hidden_in,
        cotangent,
        rest_pieces,
        (norm1_gain, norm1_bias, up_bias, down_bias, norm2_gain, norm2_bias),
    )
    shape = (rows, tokens, width)
    count = lax.axis_size("seq")
    bits = "xlhijk"[: count.bit_length() - 1]
    wide = (2,) * (len(bits) + 1) + (width // count, width)
    down_sent, down_kept, up_sent, up_kept, qkv_sent, qkv_kept = terms
    down_got = swapped(down_sent, "c").reshape(wide)
    up_got = swapped(up_sent, "c").reshape(wide)
    run = Order(smalls)
    common = (doc_offsets, doc_lengths, tokens_in, pool_kernel, saved, seq_len)
    last = len(bits)

    qkv_sent, qkv_kept, dpool_a, dq_a, dkv_a = run(
        attention_backward, grad_att.reshape(shape), qkv_sent, qkv_kept, *common, (0, 1)
    )
    down_sent, down_kept = run(split, down_kept.reshape(wide), down_got, 0, "y")
    down_got = swapped(down_sent, "y")
    up_sent, up_kept = run(split, up_kept.reshape(wide), up_got, last - 1, "l")
    up_got = swapped(up_sent, "l")
    qkv_sent, qkv_kept, dpool_b, dq_b, dkv_b = run(
        attention_backward, grad_att.reshape(shape), qkv_sent, qkv_kept, *common, (1, 2)
    )
    qkv_got = swapped(qkv_sent, "c").reshape(wide)
    small = jnp.concatenate(
        [jnp.concatenate([dpool_a, dpool_b], axis=2).reshape(10, width), smalls], axis=0
    )
    small_got = swapped(small, "c")
    down_sent, down_kept = run(split, down_kept, down_got, last - 2, "l")
    down_got = swapped(down_sent, "l")
    up_sent, up_kept = run(split, up_kept, up_got, 0, "y")
    up_got = swapped(up_sent, "y")
    dx_own, dx_ll, dx_l, dx_r = run(
        input_gradient, grad_sum1.reshape(shape), qkv_pieces, (dq_a, dq_b), (dkv_a, dkv_b)
    )
    dx_parts = (moved(dx_l, -1), moved(dx_r, 1), moved(dx_ll, -2))
    qkv_sent, qkv_kept = run(split, qkv_kept.reshape(wide), qkv_got, 0, "y")
    qkv_got = swapped(qkv_sent, "y")
    small = small + small_got
    small_got = swapped(small, "y")

    both_kept = jnp.concatenate([down_kept, up_kept], axis=-2)
    both_got = jnp.concatenate([down_got, up_got], axis=-2)
    names = ["x", *bits[2:]]
    for name in names:
        both_sent, both_kept = run(split, both_kept, both_got, both_kept.ndim - 3, name)
        both_got = swapped(both_sent, name)
    qkv_sent, qkv_kept = run(split, qkv_kept, qkv_got, last - 1, "x")
    qkv_got = swapped(qkv_sent, "x")
    small = small + small_got
    small_got = swapped(small, "x")
    (both,) = run(summed, both_kept, both_got)
    both_got = swapped(both, names[-1])
    qkv_sent, qkv_kept = run(split, qkv_kept, qkv_got, last - 2, "l")
    qkv_got = swapped(qkv_sent, "l")
    small = small + small_got
    small_got = swapped(small, "l")
    for index, name in enumerate(names[::-1]):
        (both,) = run(joined, both, both_got, both.ndim - 2, name)
        both_got = swapped(both, (names[::-1] + ["l"])[index + 1])
    for name in bits[2:]:
        qkv_sent, qkv_kept = run(split, qkv_kept, qkv_got, qkv_kept.ndim - 3, name)
        qkv_got = swapped(qkv_sent, name)
        small = small + small_got
        small_got = swapped(small, name)
    (grad_in,) = run(input_sum, dx_own, *dx_parts)
    (qkv,) = run(summed, qkv_kept, qkv_got)
    small = small + small_got
    qkv_got = swapped(qkv, bits[-1])
    (both,) = run(joined, both, both_got, both.ndim - 3, "l", F32)
    for index, name in enumerate(bits[:0:-1]):
        (qkv,) = run(joined, qkv, qkv_got, qkv.ndim - 2, name)
        qkv_got = swapped(qkv, bits[last - 2 - index])
    (qkv,) = run(joined, qkv, qkv_got, qkv.ndim - 2, "x", F32)

    def side_by_side(cells):
        parts = cells.size // (quarter * width)
        cells = cells.reshape(parts, quarter, width).transpose(1, 0, 2)
        return cells.reshape(quarter, parts * width)

    per = width // count
    both = both.reshape(count, 2, per, width)
    grad_down = both[:, 0].reshape(width, width)
    grad_up = side_by_side(both[:, 1])
    qkv = qkv.reshape(4, quarter, width)
    return (
        block_out.reshape(shape),
        grad_in,
        side_by_side(qkv[:3]),
        qkv[3],
        small[:10].reshape(2, 5, width),
        small[10],
        small[11],
        grad_up,
        small[15:].reshape(hidden),
        grad_down,
        small[12],
        small[13],
        small[14],
    )


def solution(mesh):
    placed = (
        P("dp", "seq", None),
        P("dp", "seq", None),
        P("dp", None),
        P("dp", None),
        P(),
        P(),
        P(),
        P("dp", None),
        P(),
        P("dp", None),
        P(),
        P(),
        P(),
        P("dp", None),
        P("dp", None),
    )
    return jax.shard_map(
        local,
        mesh=mesh,
        in_specs=placed,
        out_specs=(
            P("dp", "seq", None),
            P("dp", "seq", None),
            P("dp", None),
            P("dp", None),
            P(),
            P(),
            P(),
            P("dp", None),
            P(),
            P("dp", None),
            P(),
            P(),
            P(),
        ),
        check_vma=False,
    )
```

time: 776 us -> 373 us (0.48)
  blocking collectives: 340 us -> 0 us
  Pallas kernels: 0 us -> 102 us
  matrix products: 97.3 us -> 0 us
  other arithmetic: 86.6 us -> 17.9 us
  local copies, waits for them, and re-layouts: 76 us -> 29.6 us
  waiting for transfers between devices: 129 us -> 163 us
  starting transfers between devices: 26.5 us -> 51.6 us
  between operations: 15.9 us -> 1.51 us
    psum x2 -> x0, blocking collectives: 340 us -> none  [the longest x1 298 us: local(): finals = lax.psum((shares[0], shares[1], shares[2], shares[3]), 'seq')]
    ppermute x8 -> x36, waiting for transfers between devices: 26.9 us -> 163 us  [the longest x30 133 us: shifted(): return lax.ppermute(cells, axis, pairs)]
    pallas_call x0 -> x6, Pallas kernels: none -> 102 us  [the longest x2 37.9 us: attention_backward(): pl.pallas_call(partial(backward_kernel, (first, rows, tokens, width, seq_...]
    dot_general x24 -> x0, matrix products: 97.3 us -> none  [the longest x2 13.5 us: attend_backward(): jnp.einsum('rqhd,rkhd->rhqk', grad_result, value_rows, preferred_element_...]
    reduce_scatter x3 -> x0, waiting for transfers between devices: 76.8 us -> none  [the longest x1 50.6 us: local(): lax.psum_scatter(weight_terms[3].astype(jnp.bfloat16), 'dp', scatter_dime...]
    convert_element_type x9 -> x17, other arithmetic: 42.9 us -> 16.4 us  [the longest x15 14.5 us: added(): return (kept.astype(F32) + received.astype(F32)).astype(BF16)]
    all_gather x4 -> x0, waiting for transfers between devices: 25.4 us -> none  [the longest x1 25.4 us: local(): lax.all_gather(w_qkv.astype(jnp.bfloat16), 'dp', axis=0, tiled=True)]
    ppermute x8 -> x36, starting transfers between devices: 26.2 us -> 51.6 us  [the longest x30 35.2 us: shifted(): return lax.ppermute(cells, axis, pairs)]
  transfers between devices with their start and end apart: 16 -> 36, of which waited for: 7 -> 18; matrix products, arithmetic and copies ran while one was open for 24% -> 9% of each run, Pallas kernels for 0% -> 20%
where the time goes in v2:
time: 373 us; the launch traced here: 366 us
  waiting for transfers between devices  163 us (44%)
  Pallas kernels  102 us (27%)
  starting transfers between devices  51.6 us (14%)
  local copies, waits for them, and re-layouts  29.6 us (8%)
  other arithmetic  17.9 us (5%)
    ppermute x30, waiting for transfers between devices, shifted(): return lax.ppermute(cells, axis, pairs)  133 us
    pallas_call x2, Pallas kernels, attention_backward(): pl.pallas_call(partial(backward_kernel, (first, rows, tokens, width, seq_...  37.9 us
    ppermute x30, starting transfers between devices, shifted(): return lax.ppermute(cells, axis, pairs)  35.2 us
    pallas_call x1, Pallas kernels, token_part(): pl.pallas_call(token_kernel, in_specs=[whole(pltpu.VMEM)] * 3 + [whole(pl...  29.6 us
    ppermute x6, waiting for transfers between devices, moved(): return lax.ppermute(cells, 'seq', pairs)  29.6 us
    pallas_call x1, Pallas kernels, attention_forward(): pl.pallas_call(partial(forward_kernel, (rows, tokens, width, seq_len, slo...  20.4 us
    ppermute x6, starting transfers between devices, moved(): return lax.ppermute(cells, 'seq', pairs)  16.4 us
    convert_element_type x15, other arithmetic, added(): return (kept.astype(F32) + received.astype(F32)).astype(BF16)  14.5 us
  transfers between devices with their start and end apart: 36, of which 18 were waited for; matrix products, arithmetic and copies ran while one was open for 9% of the time, Pallas kernels for 20%

profile of v2, /device:TPU:0, one launch (start us, length us, event | category | flops | bytes accessed | tf_op | source)
XLA Modules:
  0.0 365.5 jit_solution(3194309909667092765)
XLA Ops:
  5.4 3.4 collective-permute-start.1
  8.9 16.1 %collective-permute-done.4.w2 = bf16[192,2304]{1,0:T(8,128)(2,1)S(1)} collective-permute-done((bf16[192,2304]{1,0:T(8,128)(2,1)S(1)}, bf16[192,2304]{1,0:T(8,128)(2,1)S(1)}, u32[]{:S(2)}, u32[]{:S(2)}) %collective-permute-start.4) | collective-permute-done | bytes 884768 | tf_op jit(solution)/shard_map/ppermute | solution.py:34
  25.9 3.7 %collective-permute-start = (bf16[2,16,768]{2,1,0:T(8,128)(2,1)S(1)}, bf16[2,16,768]{2,1,0:T(8,128)(2,1)S(1)}, u32[]{:S(2)}, u32[]{:S(2)}) collective-permute-start(bf16[2,16,768]{2,1,0:T(8,128)(2,1)S(1)} %slice.36), channel_id=1, source_target_pairs={{0,8},{4,12},{8,16},{12,20},{16,24},{20,28},{1,9},{5,13},{9,17},{1... | collective-permute-start | bytes 147464 | tf_op jit(solution)/shard_map/ppermute | solution.py:40
  37.9 17.3 %collective-permute-done.2.x_r = bf16[2,256,768]{2,1,0:T(8,128)(2,1)S(1)} collective-permute-done((bf16[2,256,768]{2,1,0:T(8,128)(2,1)S(1)}, bf16[2,256,768]{2,1,0:T(8,128)(2,1)S(1)}, u32[]{:S(2)}, u32[]{:S(2)}) %collective-permute-start.2) | collective-permute-done | bytes 786464 | tf_op jit(solution)/shard_map/ppermute | solution.py:40
  56.1 20.4 %attention_forward.1 = (bf16[2,256,768]{2,1,0:T(8,128)(2,1)}, bf16[2,784,768]{2,1,0:T(8,128)(2,1)}, bf16[2,784,768]{2,1,0:T(8,128)(2,1)}, bf16[2,192,768]{2,1,0:...) custom-call(s32[2,2]{1,0:T(2,128)} %starts_ref.5, s32[2,2]{1,0:T(2,128)} %lengths_ref.5, ...), custom_call_target="tpu_custom_call" | custom-call | flops 99999997952 | bytes 1 | tf_op jit(solution)/shard_map/attention_forward/pallas_call | solution.py:358
  76.5 19.7 %collective-permute-done.7.w2 = bf16[192,6912]{1,0:T(8,128)(2,1)} collective-permute-done((bf16[192,6912]{1,0:T(8,128)(2,1)S(1)}, bf16[192,6912]{1,0:T(8,128)(2,1)}, u32[]{:S(2)}, u32[]{:S(2)}) %collective-permute-start.7) | collective-permute-done | bytes 2654240 | tf_op jit(solution)/shard_map/ppermute | solution.py:34
  102.4 29.6 %token_part.1 = (f32[512,768]{1,0:T(8,128)}, bf16[512,768]{1,0:T(8,128)(2,1)}, f32[512,768]{1,0:T(8,128)}, bf16[2,768,768]{2,1,0:T(8,128)(2,1)}, bf16[2,768,768]...) custom-call(bf16[512,768]{1,0:T(8,128)(2,1)} %bitcast.123, ...), custom_call_target="tpu_custom_call" | custom-call | flops 99999997952 | bytes 1 | tf_op jit(solution)/shard_map/token_part/pallas_call | solution.py:834
  132.7 14.4 %attention_backward.2 = (bf16[2,4,192,768]{3,2,1,0:T(8,128)(2,1)}, bf16[2,4,192,768]{3,2,1,0:T(8,128)(2,1)}, f32[2,5,256]{2,1,0:T(8,128)}, bf16[512,256]{1,0:T(8,128)(2,1)}, bf16[2,1568,256]{2,1,0:T(8,128)(2,1)}) custom-call(s32[2,2]{1,0:T(2,128)} %starts_ref.5, s32[2,2]{1,0:T(2,128)} %lengths_ref.5, ...), custom_call_target="tpu_custom_call", output_to_operand_aliasing={{0}: (13, {}), {1}: (14, {})} | custom-call | flops 99999997952 | bytes 1 | tf_op jit(solution)/shard_map/attention_backward/pallas_call | solution.py:582
  156.1 3.3 collective-permute-start.12
  159.4 23.5 %attention_backward.3 = (bf16[2,4,192,768]{3,2,1,0:T(8,128)(2,1)}, bf16[2,4,192,768]{3,2,1,0:T(8,128)(2,1)}, f32[2,5,512]{2,1,0:T(8,128)}, bf16[512,512]{1,0:T(8,128)(2,1)}, bf16[2,1568,512]{2,1,0:T(8,128)(2,1)}) custom-call(s32[2,2]{1,0:T(2,128)} %starts_ref.5, s32[2,2]{1,0:T(2,128)} %lengths_ref.5, ...), custom_call_target="tpu_custom_call", output_to_operand_aliasing={{0}: (13, {}), {1}: (14, {})} | custom-call | flops 99999997952 | bytes 1 | tf_op jit(solution)/shard_map/attention_backward/pallas_call | solution.py:582
  188.1 11.2 %input_gradient.1 = (f32[2,256,768]{2,1,0:T(8,128)}, bf16[2,16,768]{2,1,0:T(8,128)(2,1)}, bf16[2,256,768]{2,1,0:T(8,128)(2,1)}, bf16[2,256,768]{2,1,0:T(8,128)(2,1)}) custom-call(bf16[192,2304]{1,0:T(8,128)(2,1)} %copy-done.6, bf16[192,2304]{1,0:T(8,128)(2,1)} %copy-done.17, bf16[192,2304]{1,0:T(8,128)(2,1)} %copy-done.16, ...), custom_call_target="tpu_custom_call" | custom-call | flops 99999997952 | bytes 1 | tf_op jit(solution)/shard_map/input_gradient/pallas_call | solution.py:661
  207.2 11.9 %collective-permute-done.16 = bf16[2,192,768]{2,1,0:T(8,128)(2,1)S(1)} collective-permute-done((bf16[2,192,768]{2,1,0:T(8,128)(2,1)S(1)}, bf16[2,192,768]{2,1,0:T(8,128)(2,1)S(1)}, u32[]{:S(2)}, u32[]{:S(2)}) %collective-permute-start.16) | collective-permute-done | bytes 589856 | tf_op jit(solution)/shard_map/ppermute | solution.py:34
  222.0 7.1 %collective-permute-done.17 = bf16[2,2,2,96,768]{4,3,2,1,0:T(8,128)(2,1)} collective-permute-done((bf16[2,2,2,96,768]{4,3,2,1,0:T(8,128)(2,1)}, bf16[2,2,2,96,768]{4,3,2,1,0:T(8,128)(2,1)}, u32[]{:S(2)}, u32[]{:S(2)}) %collective-permute-start.17) | collective-permute-done | bytes 1179680 | tf_op jit(solution)/shard_map/ppermute | solution.py:34
  235.4 8.4 %collective-permute-done.19 = bf16[2,2,96,768]{3,2,1,0:T(8,128)(2,1)S(1)} collective-permute-done((bf16[2,2,96,768]{3,2,1,0:T(8,128)(2,1)S(1)}, bf16[2,2,96,768]{3,2,1,0:T(8,128)(2,1)S(1)}, u32[]{:S(2)}, u32[]{:S(2)}) %collective-permute-start.19) | collective-permute-done | bytes 589856 | tf_op jit(solution)/shard_map/ppermute | solution.py:34
  243.9 5.3 %collective-permute-done.20 = bf16[192,768]{1,0:T(8,128)(2,1)S(1)} collective-permute-done((bf16[192,768]{1,0:T(8,128)(2,1)S(1)}, bf16[192,768]{1,0:T(8,128)(2,1)S(1)}, u32[]{:S(2)}, u32[]{:S(2)}) %collective-permute-start.20) | collective-permute-done | bytes 294944 | tf_op jit(solution)/shard_map/ppermute | solution.py:34
  251.5 5.4 %collective-permute-start.24 = (bf16[2,256,768]{2,1,0:T(8,128)(2,1)}, bf16[2,256,768]{2,1,0:T(8,128)(2,1)}, u32[]{:S(2)}, u32[]{:S(2)}) collective-permute-start(bf16[2,256,768]{2,1,0:T(8,128)(2,1)} %get-tuple-element.113), channel_id=1, source_target_pairs={{0,4},{4,8},{8,12},{12,16},{16,20},{20,24},{24,28},{1,5},{5,9},{9,... | collective-permute-start | bytes 2359304 | tf_op jit(solution)/shard_map/ppermute | solution.py:40
  261.0 19.8 %collective-permute-done.21 = bf16[2,192,768]{2,1,0:T(8,128)(2,1)S(1)} collective-permute-done((bf16[2,192,768]{2,1,0:T(8,128)(2,1)S(1)}, bf16[2,192,768]{2,1,0:T(8,128)(2,1)S(1)}, u32[]{:S(2)}, u32[]{:S(2)}) %collective-permute-start.21) | collective-permute-done | bytes 589856 | tf_op jit(solution)/shard_map/ppermute | solution.py:34
  282.5 12.3 %collective-permute-done.24.right = bf16[2,256,768]{2,1,0:T(8,128)(2,1)} collective-permute-done((bf16[2,256,768]{2,1,0:T(8,128)(2,1)}, bf16[2,256,768]{2,1,0:T(8,128)(2,1)}, u32[]{:S(2)}, u32[]{:S(2)}) %collective-permute-start.24) | collective-permute-done | bytes 786464 | tf_op jit(solution)/shard_map/ppermute | solution.py:40
  299.1 8.0 %collective-permute-done.27 = bf16[96,768]{1,0:T(8,128)(2,1)S(1)} collective-permute-done((bf16[96,768]{1,0:T(8,128)(2,1)S(1)}, bf16[96,768]{1,0:T(8,128)(2,1)S(1)}, u32[]{:S(2)}, u32[]{:S(2)}) %collective-permute-start.27) | collective-permute-done | bytes 147488 | tf_op jit(solution)/shard_map/ppermute | solution.py:34
  307.4 6.5 %collective-permute-done.28 = bf16[2,96,768]{2,1,0:T(8,128)(2,1)S(1)} collective-permute-done((bf16[2,96,768]{2,1,0:T(8,128)(2,1)S(1)}, bf16[2,96,768]{2,1,0:T(8,128)(2,1)S(1)}, u32[]{:S(2)}, u32[]{:S(2)}) %collective-permute-start.28) | collective-permute-done | bytes 294944 | tf_op jit(solution)/shard_map/ppermute | solution.py:34
  315.9 3.4 collective-permute-done.31
  320.7 6.3 %collective-permute-done.32 = f32[19,768]{1,0:T(8,128)S(1)} collective-permute-done((f32[19,768]{1,0:T(8,128)S(1)}, f32[19,768]{1,0:T(8,128)S(1)}, u32[]{:S(2)}, u32[]{:S(2)}) %collective-permute-start.32) | collective-permute-done | bytes 58400 | tf_op jit(solution)/shard_map/ppermute | solution.py:34
  331.4 5.0 %collective-permute-start.34 = (f32[19,768]{1,0:T(8,128)S(1)}, f32[19,768]{1,0:T(8,128)S(1)}, u32[]{:S(2)}, u32[]{:S(2)}) collective-permute-start(f32[19,768]{1,0:T(8,128)S(1)} %add.236), channel_id=1, source_target_pairs={{0,16},{4,20},{8,24},{12,28},{16,0},{20,4},{24,8},{28,12},{1,17},{... | collective-permute-start | bytes 175112 | tf_op jit(solution)/shard_map/ppermute | solution.py:34
  346.3 14.0 %collective-permute-done.35 = bf16[2,2,192,768]{3,2,1,0:T(8,128)(2,1)S(1)} collective-permute-done((bf16[2,2,192,768]{3,2,1,0:T(8,128)(2,1)S(1)}, bf16[2,2,192,768]{3,2,1,0:T(8,128)(2,1)S(1)}, u32[]{:S(2)}, u32[]{:S(2)}) %collective-permute-start.35) | collective-permute-done | bytes 1179680 | tf_op jit(solution)/shard_map/ppermute | solution.py:34
  (167 shorter events, 87.9 us)
Async XLA Ops:
  2.4 22.7 %collective-permute-start.4 = (bf16[192,2304]{1,0:T(8,128)(2,1)S(1)}, bf16[192,2304]{1,0:T(8,128)(2,1)S(1)}, u32[]{:S(2)}, u32[]{:S(2)}) collective-permute-start(bf16[192,2304]{1,0:T(8,128)(2,1)S(1)} %convert_element_type.316.w0), channel_id=1, source_target_pairs={{0,2},{1,3},{2,0},{3,1},{4,6},{5,7},{6,4},{7,5},{8,10},{9,11},{10,... | collective-permute-start | bytes 2654216 | tf_op jit(solution)/shard_map/ppermute | solution.py:34
  5.4 28.0 %collective-permute-start.1 = (bf16[2,256,768]{2,1,0:T(8,128)(2,1)}, bf16[2,256,768]{2,1,0:T(8,128)(2,1)S(1)}, u32[]{:S(2)}, u32[]{:S(2)}) collective-permute-start(bf16[2,256,768]{2,1,0:T(8,128)(2,1)} %x_own.5), channel_id=1, source_target_pairs={{0,4},{4,8},{8,12},{12,16},{16,20},{20,24},{24,28},{1,5},{5,9},{9,... | collective-permute-start | bytes 2359304 | tf_op jit(solution)/shard_map/ppermute | solution.py:40
  8.9 29.1 %collective-permute-start.3 = (bf16[192,2304]{1,0:T(8,128)(2,1)S(1)}, bf16[192,2304]{1,0:T(8,128)(2,1)S(1)}, u32[]{:S(2)}, u32[]{:S(2)}) collective-permute-start(bf16[192,2304]{1,0:T(8,128)(2,1)S(1)} %convert_element_type.316.w0), channel_id=1, source_target_pairs={{0,1},{1,0},{2,3},{3,2},{4,5},{5,4},{6,7},{7,6},{8,9},{9,8},{10,11... | collective-permute-start | bytes 2654216 | tf_op jit(solution)/shard_map/ppermute | solution.py:34
  25.1 31.0 %collective-permute-start.5 = (bf16[192,2304]{1,0:T(8,128)(2,1)S(1)}, bf16[192,2304]{1,0:T(8,128)(2,1)}, u32[]{:S(2)}, u32[]{:S(2)}) collective-permute-start(bf16[192,2304]{1,0:T(8,128)(2,1)S(1)} %collective-permute-done.4.w2), channel_id=1, source_target_pairs={{0,1},{1,0},{2,3},{3,2},{4,5},{5,4},{6,7},{7,6},{8,9},{9,8},{10,11... | collective-permute-start | bytes 2654216 | tf_op jit(solution)/shard_map/ppermute | solution.py:34
  33.7 21.5 %collective-permute-start.2 = (bf16[2,256,768]{2,1,0:T(8,128)(2,1)S(1)}, bf16[2,256,768]{2,1,0:T(8,128)(2,1)S(1)}, u32[]{:S(2)}, u32[]{:S(2)}) collective-permute-start(bf16[2,256,768]{2,1,0:T(8,128)(2,1)S(1)} %copy-done.15), channel_id=1, source_target_pairs={{4,0},{8,4},{12,8},{16,12},{20,16},{24,20},{28,24},{5,1},{9,5},{13... | collective-permute-start | bytes 2359304 | tf_op jit(solution)/shard_map/ppermute | solution.py:40
  36.4 59.8 %collective-permute-start.7 = (bf16[192,6912]{1,0:T(8,128)(2,1)S(1)}, bf16[192,6912]{1,0:T(8,128)(2,1)}, u32[]{:S(2)}, u32[]{:S(2)}) collective-permute-start(bf16[192,6912]{1,0:T(8,128)(2,1)S(1)} %pad_maximum_fusion.w0), channel_id=1, source_target_pairs={{0,2},{1,3},{2,0},{3,1},{4,6},{5,7},{6,4},{7,5},{8,10},{9,11},{10,... | collective-permute-start | bytes 7962632 | tf_op jit(solution)/shard_map/ppermute | solution.py:34
  37.9 64.5 %collective-permute-start.6 = (bf16[192,6912]{1,0:T(8,128)(2,1)S(1)}, bf16[192,6912]{1,0:T(8,128)(2,1)}, u32[]{:S(2)}, u32[]{:S(2)}) collective-permute-start(bf16[192,6912]{1,0:T(8,128)(2,1)S(1)} %pad_maximum_fusion.w0), channel_id=1, source_target_pairs={{0,1},{1,0},{2,3},{3,2},{4,5},{5,4},{6,7},{7,6},{8,9},{9,8},{10,11... | collective-permute-start | bytes 7962632 | tf_op jit(solution)/shard_map/ppermute | solution.py:34
  132.1 15.1 %collective-permute-start.9 = (bf16[2,768,768]{2,1,0:T(8,128)(2,1)}, bf16[2,768,768]{2,1,0:T(8,128)(2,1)}, u32[]{:S(2)}, u32[]{:S(2)}) collective-permute-start(bf16[2,768,768]{2,1,0:T(8,128)(2,1)} %get-tuple-element.87), channel_id=1, source_target_pairs={{0,1},{1,0},{2,3},{3,2},{4,5},{5,4},{6,7},{7,6},{8,9},{9,8},{10,11... | collective-permute-start | bytes 7077896 | tf_op jit(solution)/shard_map/ppermute | solution.py:34
  132.6 20.1 %collective-permute-start.10 = (bf16[2,768,768]{2,1,0:T(8,128)(2,1)}, bf16[2,768,768]{2,1,0:T(8,128)(2,1)S(1)}, u32[]{:S(2)}, u32[]{:S(2)}) collective-permute-start(bf16[2,768,768]{2,1,0:T(8,128)(2,1)} %get-tuple-element.89), channel_id=1, source_target_pairs={{0,1},{1,0},{2,3},{3,2},{4,5},{5,4},{6,7},{7,6},{8,9},{9,8},{10,11... | collective-permute-start | bytes 7077896 | tf_op jit(solution)/shard_map/ppermute | solution.py:34
  151.2 31.8 %collective-permute-start.11 = (bf16[2,2,2,96,768]{4,3,0,2,1:T(8,128)(2,1)}, bf16[2,2,2,96,768]{4,3,0,2,1:T(8,128)(2,1)}, u32[]{:S(2)}, u32[]{:S(2)}) collective-permute-start(bf16[2,2,2,96,768]{4,3,0,2,1:T(8,128)(2,1)} %get-tuple-element.150), channel_id=1, source_target_pairs={{0,2},{1,3},{2,0},{3,1},{4,6},{5,7},{6,4},{7,5},{8,10},{9,11},{10,... | collective-permute-start | bytes 3538952 | tf_op jit(solution)/shard_map/ppermute | solution.py:34
  156.1 29.8 %collective-permute-start.12 = (bf16[2,2,2,96,768]{4,3,1,2,0:T(8,128)(2,1)}, bf16[2,2,2,96,768]{4,3,1,2,0:T(8,128)(2,1)S(1)}, u32[]{:S(2)}, u32[]{:S(2)}) collective-permute-start(bf16[2,2,2,96,768]{4,3,1,2,0:T(8,128)(2,1)} %get-tuple-element.154), channel_id=1, source_target_pairs={{0,8},{4,12},{8,0},{12,4},{16,24},{20,28},{24,16},{28,20},{1,9},{5... | collective-permute-start | bytes 3538952 | tf_op jit(solution)/shard_map/ppermute | solution.py:34
  182.9 16.4 %collective-permute-start.13 = (bf16[2,4,192,768]{3,2,1,0:T(8,128)(2,1)}, bf16[2,4,192,768]{3,2,1,0:T(8,128)(2,1)}, u32[]{:S(2)}, u32[]{:S(2)}) collective-permute-start(bf16[2,4,192,768]{3,2,1,0:T(8,128)(2,1)} %get-tuple-element.96), channel_id=1, source_target_pairs={{0,1},{1,0},{2,3},{3,2},{4,5},{5,4},{6,7},{7,6},{8,9},{9,8},{10,11... | collective-permute-start | bytes 7077896 | tf_op jit(solution)/shard_map/ppermute | solution.py:34
  185.4 17.5 %collective-permute-start.14 = (bf16[2,2,96,768]{3,2,0,1:T(8,128)(2,1)}, bf16[2,2,96,768]{3,2,0,1:T(8,128)(2,1)S(1)}, u32[]{:S(2)}, u32[]{:S(2)}) collective-permute-start(bf16[2,2,96,768]{3,2,0,1:T(8,128)(2,1)} %get-tuple-element.146), channel_id=1, source_target_pairs={{0,8},{4,12},{8,0},{12,4},{16,24},{20,28},{24,16},{28,20},{1,9},{5... | collective-permute-start | bytes 1769480 | tf_op jit(solution)/shard_map/ppermute | solution.py:34
  187.0 15.9 %collective-permute-start.15 = (bf16[2,2,96,768]{3,2,0,1:T(8,128)(2,1)}, bf16[2,2,96,768]{3,2,0,1:T(8,128)(2,1)}, u32[]{:S(2)}, u32[]{:S(2)}) collective-permute-start(bf16[2,2,96,768]{3,2,0,1:T(8,128)(2,1)} %get-tuple-element.148), channel_id=1, source_target_pairs={{0,2},{1,3},{2,0},{3,1},{4,6},{5,7},{6,4},{7,5},{8,10},{9,11},{10,... | collective-permute-start | bytes 1769480 | tf_op jit(solution)/shard_map/ppermute | solution.py:34
  201.9 27.3 %collective-permute-start.17 = (bf16[2,2,2,96,768]{4,3,2,1,0:T(8,128)(2,1)}, bf16[2,2,2,96,768]{4,3,2,1,0:T(8,128)(2,1)}, u32[]{:S(2)}, u32[]{:S(2)}) collective-permute-start(bf16[2,2,2,96,768]{4,3,2,1,0:T(8,128)(2,1)} %fusion.5), channel_id=1, source_target_pairs={{0,2},{1,3},{2,0},{3,1},{4,6},{5,7},{6,4},{7,5},{8,10},{9,11},{10,... | collective-permute-start | bytes 3538952 | tf_op jit(solution)/shard_map/ppermute | solution.py:34
  234.1 15.1 %collective-permute-start.20 = (bf16[192,768]{1,0:T(8,128)(2,1)S(1)}, bf16[192,768]{1,0:T(8,128)(2,1)S(1)}, u32[]{:S(2)}, u32[]{:S(2)}) collective-permute-start(bf16[192,768]{1,0:T(8,128)(2,1)S(1)} %add_convert_fusion.14), channel_id=1, source_target_pairs={{0,16},{4,20},{8,24},{12,28},{16,0},{20,4},{24,8},{28,12},{1,17},{... | collective-permute-start | bytes 884744 | tf_op jit(solution)/shard_map/ppermute | solution.py:34
  249.4 31.4 %collective-permute-start.21 = (bf16[2,192,768]{2,1,0:T(8,128)(2,1)S(1)}, bf16[2,192,768]{2,1,0:T(8,128)(2,1)S(1)}, u32[]{:S(2)}, u32[]{:S(2)}) collective-permute-start(bf16[2,192,768]{2,1,0:T(8,128)(2,1)S(1)} %pad_maximum_fusion.4), channel_id=1, source_target_pairs={{0,4},{4,0},{8,12},{12,8},{16,20},{20,16},{24,28},{28,24},{1,5},{5... | collective-permute-start | bytes 1769480 | tf_op jit(solution)/shard_map/ppermute | solution.py:34
  250.2 32.3 %collective-permute-start.23 = (bf16[2,256,768]{2,1,0:T(8,128)(2,1)}, bf16[2,256,768]{2,1,0:T(8,128)(2,1)}, u32[]{:S(2)}, u32[]{:S(2)}) collective-permute-start(bf16[2,256,768]{2,1,0:T(8,128)(2,1)} %get-tuple-element.112), channel_id=1, source_target_pairs={{4,0},{8,4},{12,8},{16,12},{20,16},{24,20},{28,24},{5,1},{9,5},{13... | collective-permute-start | bytes 2359304 | tf_op jit(solution)/shard_map/ppermute | solution.py:40
  251.5 43.3 %collective-permute-start.24 = (bf16[2,256,768]{2,1,0:T(8,128)(2,1)}, bf16[2,256,768]{2,1,0:T(8,128)(2,1)}, u32[]{:S(2)}, u32[]{:S(2)}) collective-permute-start(bf16[2,256,768]{2,1,0:T(8,128)(2,1)} %get-tuple-element.113), channel_id=1, source_target_pairs={{0,4},{4,8},{8,12},{12,16},{16,20},{20,24},{24,28},{1,5},{5,9},{9,... | collective-permute-start | bytes 2359304 | tf_op jit(solution)/shard_map/ppermute | solution.py:40
  256.9 25.6 %collective-permute-start.25 = (bf16[2,16,768]{2,1,0:T(8,128)(2,1)S(1)}, bf16[2,16,768]{2,1,0:T(8,128)(2,1)S(1)}, u32[]{:S(2)}, u32[]{:S(2)}) collective-permute-start(bf16[2,16,768]{2,1,0:T(8,128)(2,1)S(1)} %copy-done.21), channel_id=1, source_target_pairs={{8,0},{12,4},{16,8},{20,12},{24,16},{28,20},{9,1},{13,5},{17,9},{2... | collective-permute-start | bytes 147464 | tf_op jit(solution)/shard_map/ppermute | solution.py:40
  258.2 22.8 %collective-permute-start.22 = (bf16[2,96,768]{2,1,0:T(8,128)(2,1)S(1)}, bf16[2,96,768]{2,1,0:T(8,128)(2,1)S(1)}, u32[]{:S(2)}, u32[]{:S(2)}) collective-permute-start(bf16[2,96,768]{2,1,0:T(8,128)(2,1)S(1)} %fusion.19), channel_id=1, source_target_pairs={{0,8},{4,12},{8,0},{12,4},{16,24},{20,28},{24,16},{28,20},{1,9},{5... | collective-permute-start | bytes 884744 | tf_op jit(solution)/shard_map/ppermute | solution.py:34
  281.1 16.6 %collective-permute-start.26 = (bf16[96,768]{1,0:T(8,128)(2,1)S(1)}, bf16[96,768]{1,0:T(8,128)(2,1)S(1)}, u32[]{:S(2)}, u32[]{:S(2)}) collective-permute-start(bf16[96,768]{1,0:T(8,128)(2,1)S(1)} %get-tuple-element.166), channel_id=1, source_target_pairs={{0,16},{4,20},{8,24},{12,28},{16,0},{20,4},{24,8},{28,12},{1,17},{... | collective-permute-start | bytes 442376 | tf_op jit(solution)/shard_map/ppermute | solution.py:34
  314.1 30.8 %collective-permute-start.29 = (bf16[2,2,96,768]{3,2,0,1:T(8,128)(2,1)S(1)}, bf16[2,2,96,768]{3,2,0,1:T(8,128)(2,1)S(1)}, u32[]{:S(2)}, u32[]{:S(2)}) collective-permute-start(bf16[2,2,96,768]{3,2,0,1:T(8,128)(2,1)S(1)} %pad_maximum_fusion.5), channel_id=1, source_target_pairs={{0,4},{4,0},{8,12},{12,8},{16,20},{20,16},{24,28},{28,24},{1,5},{5... | collective-permute-start | bytes 1769480 | tf_op jit(solution)/shard_map/ppermute | solution.py:34
  336.4 23.8 %collective-permute-start.35 = (bf16[2,2,192,768]{3,2,1,0:T(8,128)(2,1)S(1)}, bf16[2,2,192,768]{3,2,1,0:T(8,128)(2,1)S(1)}, u32[]{:S(2)}, u32[]{:S(2)}) collective-permute-start(bf16[2,2,192,768]{3,2,1,0:T(8,128)(2,1)S(1)} %pad_maximum_fusion.3), channel_id=1, source_target_pairs={{0,8},{4,12},{8,0},{12,4},{16,24},{20,28},{24,16},{28,20},{1,9},{5... | collective-permute-start | bytes 3538952 | tf_op jit(solution)/shard_map/ppermute | solution.py:34
  (35 other events, 443.5 us)
